TPU v7x, 32 devices: a whole 2x2x4 slice. The times are simulated.
32 devices in a mesh: batch: 8 (over y, x, core), height: 4 (over z).
Axes of the slice: x: 2, y: 2, z: 4, core: 2. Of those that a mesh axis runs over, the one named last changes fastest.
Arguments:
- images: bfloat16 [192, 32, 32, 1024], P('batch', 'height'), may hold values from -8 to 8
- w_first: bfloat16 [1024, 1024], replicated, may hold values from -0.1875 to 0.1875
- gain_first: float32 [1024], replicated, may hold values from 0.25 to 1.75
- shift_first: float32 [1024], replicated, may hold values from -3 to 3
- w_mid: bfloat16 [3, 3, 32, 1024], replicated, may hold values from -0.375 to 0.375
- gain_mid: float32 [1024], replicated, may hold values from 0.25 to 1.75
- shift_mid: float32 [1024], replicated, may hold values from -3 to 3
- w_last: bfloat16 [1024, 2048], replicated, may hold values from -0.1875 to 0.1875
- gain_last: float32 [2048], replicated, may hold values from 0.25 to 1.75
- shift_last: float32 [2048], replicated, may hold values from -3 to 3
- w_side: bfloat16 [1024, 2048], replicated, may hold values from -0.1875 to 0.1875
- gain_side: float32 [2048], replicated, may hold values from 0.25 to 1.75
- shift_side: float32 [2048], replicated, may hold values from -3 to 3
- cotangent: bfloat16 [192, 16, 16, 2048], P('batch', 'height'), may hold values from -6 to 6
Outputs:
- output: bfloat16 [192, 16, 16, 2048], P('batch', 'height')
- grad_images: bfloat16 [192, 32, 32, 1024], P('batch', 'height')
- grad_first: float32 [1024, 1024], replicated
- grad_gain_first: float32 [1024], replicated
- grad_shift_first: float32 [1024], replicated
- grad_mid: float32 [3, 3, 32, 1024], replicated
- grad_gain_mid: float32 [1024], replicated
- grad_shift_mid: float32 [1024], replicated
- grad_last: float32 [1024, 2048], replicated
- grad_gain_last: float32 [2048], replicated
- grad_shift_last: float32 [2048], replicated
- grad_side: float32 [1024, 2048], replicated
- grad_gain_side: float32 [2048], replicated
- grad_shift_side: float32 [2048], replicated
All inputs are finite; a program needn't handle non-finite values.
Results may differ from a plain program's by a relative error of at most 0.0084.
Values may be sent and summed in bfloat16 or wider, within the bound.
A program may use at most 704 MiB of HBM per device.

v0:
```python
import jax
import jax.numpy as jnp
from jax import lax
from jax.sharding import PartitionSpec as P

C_IN = 1024
MID = 1024
C_OUT = 2048
GROUPS = 32
W_IN = 32
GW = 32


EPSILON = 1e-05


def shifted(array, axis, by):
    size = lax.axis_size(axis)
    pairs = [(i, i + by) for i in range(size) if 0 <= i + by < size]
    return lax.ppermute(array, axis, pairs)


def moments(values):
    return (jnp.sum(values, axis=0), jnp.sum(values * values, axis=0))


def normalize(values, totals_sum, totals_square, cell_total):
    average = totals_sum / cell_total
    inverse = lax.rsqrt(totals_square / cell_total - average * average + EPSILON)
    return ((values - average) * inverse, inverse)


def norm_back(upstream, normed, gain_vec, inverse, total_up, total_cross, cell_total):
    return (
        gain_vec
        * inverse
        * (upstream - total_up / cell_total - normed * (total_cross / cell_total))
    )


def silu_slope(values):
    sigma = jax.nn.sigmoid(values)
    return sigma * (1.0 + values * (1.0 - sigma))


def per_device(
    images,
    w_first,
    gain_first,
    shift_first,
    w_mid,
    gain_mid,
    shift_mid,
    w_last,
    gain_last,
    shift_last,
    w_side,
    gain_side,
    shift_side,
    cotangent,
):
    img_count = images.shape[0]
    rows_in = images.shape[1]
    rows_out = rows_in // 2
    cols_out = W_IN // 2
    cell_in = float(img_count * rows_in * W_IN * lax.axis_size("batch") * lax.axis_size("height"))
    cell_out = cell_in / 4.0
    flat_in = images.reshape(-1, C_IN)
    side_in = images[:, ::2, ::2, :].reshape(-1, C_IN)
    first_pre = jnp.dot(flat_in, w_first, preferred_element_type=jnp.float32)
    first_terms = jnp.concatenate(moments(first_pre))
    first_totals = lax.psum(first_terms, ("batch", "height"))
    first_normed, first_inverse = normalize(
        first_pre, first_totals[:MID], first_totals[MID : 2 * MID], cell_in
    )
    first_act = jax.nn.silu(gain_first * first_normed + shift_first).astype(jnp.bfloat16)
    first_grid = first_act.reshape(img_count, rows_in, W_IN, MID)
    upper_row = shifted(first_grid[:, rows_in - 1], "height", 1)
    padded = jnp.pad(
        jnp.concatenate([upper_row[:, None], first_grid], axis=1), ((0, 0), (0, 1), (1, 1), (0, 0))
    )
    mid_pre = jnp.zeros((img_count, rows_out, cols_out, GROUPS, GW), jnp.float32)
    for tap_row in range(3):
        for tap_col in range(3):
            window = padded[:, tap_row : tap_row + rows_in : 2, tap_col : tap_col + W_IN : 2, :]
            window = window.reshape(img_count, rows_out, cols_out, GROUPS, GW)
            kernel = w_mid[tap_row, tap_col].reshape(GW, GROUPS, GW)
            mid_pre = mid_pre + jnp.einsum(
                "bhwgc,cgo->bhwgo", window, kernel, preferred_element_type=jnp.float32
            )
    mid_flat = mid_pre.reshape(-1, MID)
    mid_totals = lax.psum(jnp.concatenate(moments(mid_flat)), ("batch", "height"))
    mid_normed, mid_inverse = normalize(mid_flat, mid_totals[:MID], mid_totals[MID:], cell_out)
    mid_act = jax.nn.silu(gain_mid * mid_normed + shift_mid).astype(jnp.bfloat16)
    last_pre = jnp.dot(mid_act, w_last, preferred_element_type=jnp.float32)
    side_pre = jnp.dot(side_in, w_side, preferred_element_type=jnp.float32)
    last_terms = jnp.concatenate(moments(last_pre) + moments(side_pre))
    last_totals = lax.psum(last_terms, ("batch", "height"))
    last_normed, last_inverse = normalize(
        last_pre, last_totals[:C_OUT], last_totals[C_OUT : 2 * C_OUT], cell_out
    )
    side_totals = last_totals[2 * C_OUT :]
    side_normed, side_inverse = normalize(
        side_pre, side_totals[:C_OUT], side_totals[C_OUT:], cell_out
    )
    summed = gain_last * last_normed + shift_last + gain_side * side_normed + shift_side
    output = jax.nn.silu(summed).astype(jnp.bfloat16).reshape(img_count, rows_out, cols_out, C_OUT)
    upstream = cotangent.reshape(-1, C_OUT).astype(jnp.float32) * silu_slope(summed)
    back_terms = jnp.concatenate(
        [
            jnp.sum(upstream, axis=0),
            jnp.sum(upstream * last_normed, axis=0),
            jnp.sum(upstream * side_normed, axis=0),
        ]
    )
    back_totals = lax.psum(back_terms, ("batch", "height"))
    total_up = back_totals[:C_OUT]
    last_cross = back_totals[C_OUT : 2 * C_OUT]
    side_cross = back_totals[2 * C_OUT :]
    last_grad = norm_back(
        upstream, last_normed, gain_last, last_inverse, total_up, last_cross, cell_out
    ).astype(jnp.bfloat16)
    side_grad = norm_back(
        upstream, side_normed, gain_side, side_inverse, total_up, side_cross, cell_out
    ).astype(jnp.bfloat16)
    grad_last_local = jnp.einsum(
        "pm,po->mo", mid_act, last_grad, preferred_element_type=jnp.float32
    )
    grad_side_local = jnp.einsum(
        "pc,po->co", side_in, side_grad, preferred_element_type=jnp.float32
    )
    tail_flat = jnp.concatenate([grad_last_local.reshape(-1), grad_side_local.reshape(-1)])
    mid_up = jnp.dot(last_grad, w_last.T, preferred_element_type=jnp.float32)
    side_back = jnp.dot(side_grad, w_side.T, preferred_element_type=jnp.float32)
    mid_up = mid_up * silu_slope(gain_mid * mid_normed + shift_mid)
    mid_back = lax.psum(
        jnp.concatenate([jnp.sum(mid_up, axis=0), jnp.sum(mid_up * mid_normed, axis=0)]),
        ("batch", "height"),
    )
    mid_grad = norm_back(
        mid_up, mid_normed, gain_mid, mid_inverse, mid_back[:MID], mid_back[MID:], cell_out
    )
    mid_grad = mid_grad.astype(jnp.bfloat16).reshape(img_count, rows_out, cols_out, GROUPS, GW)
    zero_part = jnp.zeros((img_count, rows_out + 1, cols_out + 1, MID), jnp.float32)
    parity_sums = [[zero_part, zero_part], [zero_part, zero_part]]
    kernel_grads = []
    for tap_row in range(3):
        for tap_col in range(3):
            window = padded[:, tap_row : tap_row + rows_in : 2, tap_col : tap_col + W_IN : 2, :]
            window = window.reshape(img_count, rows_out, cols_out, GROUPS, GW)
            kernel = w_mid[tap_row, tap_col].reshape(GW, GROUPS, GW)
            kernel_grads.append(
                jnp.einsum(
                    "bhwgc,bhwgo->cgo", window, mid_grad, preferred_element_type=jnp.float32
                ).reshape(GW, MID)
            )
            tap_grad = jnp.einsum(
                "bhwgo,cgo->bhwgc", mid_grad, kernel, preferred_element_type=jnp.float32
            ).reshape(img_count, rows_out, cols_out, MID)
            placed = jnp.pad(
                tap_grad,
                (
                    (0, 0),
                    (tap_row // 2, 1 - tap_row // 2),
                    (tap_col // 2, 1 - tap_col // 2),
                    (0, 0),
                ),
            )
            parity_sums[tap_row % 2][tap_col % 2] = parity_sums[tap_row % 2][tap_col % 2] + placed
    grad_mid_local = jnp.stack(kernel_grads).reshape(3, 3, GW, MID)
    even_rows = jnp.stack([parity_sums[0][0], parity_sums[0][1]], axis=3).reshape(
        img_count, rows_out + 1, W_IN + 2, MID
    )
    odd_rows = jnp.stack([parity_sums[1][0], parity_sums[1][1]], axis=3).reshape(
        img_count, rows_out + 1, W_IN + 2, MID
    )
    grad_grid = jnp.stack([even_rows, odd_rows], axis=2).reshape(
        img_count, rows_in + 2, W_IN + 2, MID
    )
    edge_grad = grad_grid[:, 0, 1 : W_IN + 1]
    from_below = shifted(edge_grad.astype(jnp.bfloat16), "height", -1).astype(edge_grad.dtype)
    first_up = grad_grid[:, 1 : rows_in + 1, 1 : W_IN + 1] + jnp.pad(
        from_below[:, None], ((0, 0), (rows_in - 1, 0), (0, 0), (0, 0))
    )
    first_up = first_up.reshape(-1, MID)
    first_up = first_up * silu_slope(gain_first * first_normed + shift_first)
    first_back = lax.psum(
        jnp.concatenate([jnp.sum(first_up, axis=0), jnp.sum(first_up * first_normed, axis=0)]),
        ("batch", "height"),
    )
    first_grad = norm_back(
        first_up,
        first_normed,
        gain_first,
        first_inverse,
        first_back[:MID],
        first_back[MID:],
        cell_in,
    ).astype(jnp.bfloat16)
    grad_first_local = jnp.einsum(
        "pc,pm->cm", flat_in, first_grad, preferred_element_type=jnp.float32
    )
    main_back = jnp.dot(first_grad, w_first.T, preferred_element_type=jnp.float32)
    side_grid = side_back.reshape(img_count, rows_out, cols_out, C_IN)
    spaced = jnp.stack([side_grid, jnp.zeros_like(side_grid)], axis=3).reshape(
        img_count, rows_out, W_IN, C_IN
    )
    spaced = jnp.stack([spaced, jnp.zeros_like(spaced)], axis=2).reshape(
        img_count, rows_in, W_IN, C_IN
    )
    grad_images = (main_back.reshape(img_count, rows_in, W_IN, C_IN) + spaced).astype(jnp.bfloat16)
    head_flat = jnp.concatenate([grad_first_local.reshape(-1), grad_mid_local.reshape(-1)])
    grad_flat = jnp.concatenate([head_flat, tail_flat])
    shard_sum = lax.psum_scatter(grad_flat, ("batch", "height"), scatter_dimension=0, tiled=True)
    gathered = lax.all_gather(
        shard_sum.astype(jnp.bfloat16), ("batch", "height"), axis=0, tiled=True
    ).astype(shard_sum.dtype)
    size_first = C_IN * MID
    size_mid = 9 * GW * MID
    size_last = MID * C_OUT
    tail_all = gathered[size_first + size_mid :]
    grad_first = gathered[:size_first].reshape(C_IN, MID)
    grad_mid = gathered[size_first : size_first + size_mid].reshape(3, 3, GW, MID)
    grad_last = tail_all[:size_last].reshape(MID, C_OUT)
    grad_side = tail_all[size_last:].reshape(C_IN, C_OUT)
    return (
        output,
        grad_images,
        grad_first,
        first_back[MID:],
        first_back[:MID],
        grad_mid,
        mid_back[MID:],
        mid_back[:MID],
        grad_last,
        last_cross,
        total_up,
        grad_side,
        side_cross,
        total_up,
    )


def solution(mesh):
    in_specs = (
        P("batch", "height", None, None),
        P(),
        P(),
        P(),
        P(),
        P(),
        P(),
        P(),
        P(),
        P(),
        P(),
        P(),
        P(),
        P("batch", "height", None, None),
    )
    out_specs = (
        P("batch", "height", None, None),
        P("batch", "height", None, None),
        P(),
        P(),
        P(),
        P(),
        P(),
        P(),
        P(),
        P(),
        P(),
        P(),
        P(),
        P(),
    )
    return jax.shard_map(
        per_device, mesh=mesh, in_specs=in_specs, out_specs=out_specs, check_vma=False
    )
```

profile of v0, /device:TPU:0, one launch (start us, length us, event | category | flops | bytes accessed | tf_op | source)
XLA Modules:
  0.0 3287.8 jit_solution(2416066297466152101)
XLA Ops:
  30.0 42.0 %psum.42 = f32[2048]{0:T(1024)S(1)} all-reduce(f32[2048]{0:T(1024)S(1)} %pad_maximum_fusion.6), channel_id=1, replica_groups=mesh['batch'=8,'height'=4] {'batch','height'}, use_global_device_ids=true, to_apply=%region_2.0 | all-reduce | flops 2048 | bytes 16384 | tf_op jit(solution)/shard_map/psum | solution.py:72
  95.5 51.0 %slice.205 = bf16[24,4,16,1024]{3,2,1,0:T(8,128)(2,1)} slice(bf16[24,8,32,1024]{3,2,1,0:T(8,128)(2,1)} %param.14), slice={[0:24:1], [0:8:2], [0:32:2], [0:1024:1]} | slice | bytes 6291456 | tf_op jit(solution)/shard_map/slice | solution.py:69
  185.3 51.0 %slice.199 = bf16[24,4,16,1024]{3,2,1,0:T(8,128)(2,1)} slice(bf16[24,10,34,1024]{3,2,1,0:T(8,128)(2,1)} %fusion.5), slice={[0:24:1], [2:10:2], [1:33:2], [0:1024:1]} | slice | bytes 6291456 | tf_op jit(solution)/shard_map/slice | solution.py:85
  236.3 51.0 %slice.197 = bf16[24,4,16,1024]{3,2,1,0:T(8,128)(2,1)} slice(bf16[24,10,34,1024]{3,2,1,0:T(8,128)(2,1)} %fusion.5), slice={[0:24:1], [2:10:2], [0:32:2], [0:1024:1]} | slice | bytes 6291456 | tf_op jit(solution)/shard_map/slice | solution.py:85
  287.3 51.4 %slice.195 = bf16[24,4,16,1024]{3,2,1,0:T(8,128)(2,1)} slice(bf16[24,10,34,1024]{3,2,1,0:T(8,128)(2,1)} %fusion.5), slice={[0:24:1], [1:9:2], [2:34:2], [0:1024:1]} | slice | bytes 6291456 | tf_op jit(solution)/shard_map/slice | solution.py:85
  338.7 50.6 %slice.193 = bf16[24,4,16,1024]{3,2,1,0:T(8,128)(2,1)} slice(bf16[24,10,34,1024]{3,2,1,0:T(8,128)(2,1)} %fusion.5), slice={[0:24:1], [1:9:2], [1:33:2], [0:1024:1]} | slice | bytes 6291456 | tf_op jit(solution)/shard_map/slice | solution.py:85
  389.3 50.6 %slice.191 = bf16[24,4,16,1024]{3,2,1,0:T(8,128)(2,1)} slice(bf16[24,10,34,1024]{3,2,1,0:T(8,128)(2,1)} %fusion.5), slice={[0:24:1], [1:9:2], [0:32:2], [0:1024:1]} | slice | bytes 6291456 | tf_op jit(solution)/shard_map/slice | solution.py:85
  439.9 51.4 %slice.189 = bf16[24,4,16,1024]{3,2,1,0:T(8,128)(2,1)} slice(bf16[24,10,34,1024]{3,2,1,0:T(8,128)(2,1)} %fusion.5), slice={[0:24:1], [0:8:2], [2:34:2], [0:1024:1]} | slice | bytes 6291456 | tf_op jit(solution)/shard_map/slice | solution.py:85
  491.3 50.6 %slice.187 = bf16[24,4,16,1024]{3,2,1,0:T(8,128)(2,1)} slice(bf16[24,10,34,1024]{3,2,1,0:T(8,128)(2,1)} %fusion.5), slice={[0:24:1], [0:8:2], [1:33:2], [0:1024:1]} | slice | bytes 6291456 | tf_op jit(solution)/shard_map/slice | solution.py:85
  541.9 50.6 %slice.185 = bf16[24,4,16,1024]{3,2,1,0:T(8,128)(2,1)} slice(bf16[24,10,34,1024]{3,2,1,0:T(8,128)(2,1)} %fusion.5), slice={[0:24:1], [0:8:2], [0:32:2], [0:1024:1]} | slice | bytes 6291456 | tf_op jit(solution)/shard_map/slice | solution.py:85
  592.4 51.8 %slice.201 = bf16[24,4,16,1024]{3,2,1,0:T(8,128)(2,1)} slice(bf16[24,10,34,1024]{3,2,1,0:T(8,128)(2,1)} %fusion.5), slice={[0:24:1], [2:10:2], [2:34:2], [0:1024:1]} | slice | bytes 6291456 | tf_op jit(solution)/shard_map/slice | solution.py:85
  967.2 80.8 %fusion.98 = (f32[32,32]{1,0:T(8,128)S(1)}, f32[32,32]{1,0:T(8,128)S(1)}, f32[24,4,16,32,32]{4,0,2,1,3:T(8,128)}) fusion(f32[32,24,4,16,32]{4,1,3,2,0:T(8,128)} %fusion.9, f32[32,24,4,16,32]{4,1,3,2,0:T(8,128)} %fusion.13, f32[32,24,4,16,32]{4,1,3,2,0:T(8,128)} %fusion.17, f32[32,24,4,16,32]{4,1,3,2,0:T(8,128)} %fusion.21, ...), kind=kLoop, calls=%fused_computation.188 | loop fusion | flops 17299456 | bytes 62922752 | tf_op jit(solution)/shard_map/reduce_sum | solution.py:24
  1048.1 38.7 %psum.43 = f32[2048]{0:T(1024)S(1)} all-reduce(f32[2048]{0:T(1024)S(1)} %pad_maximum_fusion.7), channel_id=1, replica_groups=mesh['batch'=8,'height'=4] {'batch','height'}, use_global_device_ids=true, to_apply=%region_5.6 | all-reduce | flops 2048 | bytes 16384 | tf_op jit(solution)/shard_map/psum | solution.py:92
  1145.2 41.7 %psum.44 = f32[8192]{0:T(1024)S(1)} all-reduce(f32[8192]{0:T(1024)S(1)} %pad_maximum_fusion.4), channel_id=1, replica_groups=mesh['batch'=8,'height'=4] {'batch','height'}, use_global_device_ids=true, to_apply=%region_10.11 | all-reduce | flops 8192 | bytes 65536 | tf_op jit(solution)/shard_map/psum | solution.py:98
  1207.3 38.9 %psum.45 = f32[6144]{0:T(1024)S(1)} all-reduce(f32[6144]{0:T(1024)S(1)} %pad_maximum_fusion.5), channel_id=1, replica_groups=mesh['batch'=8,'height'=4] {'batch','height'}, use_global_device_ids=true, to_apply=%region_14.15 | all-reduce | flops 6144 | bytes 49152 | tf_op jit(solution)/shard_map/psum | solution.py:116
  1277.4 41.4 %psum.46 = f32[2048]{0:T(1024)S(1)} all-reduce(f32[2048]{0:T(1024)S(1)} %pad_maximum_fusion.8), channel_id=1, replica_groups=mesh['batch'=8,'height'=4] {'batch','height'}, use_global_device_ids=true, to_apply=%region_17.18 | all-reduce | flops 2048 | bytes 16384 | tf_op jit(solution)/shard_map/psum | solution.py:136
  1343.2 42.5 %fusion.39 = f32[32,32,32,1,1]{2,1,4,3,0:T(8,128)} fusion(bf16[24,4,16,32,32]{4,3,2,1,0:T(8,128)(2,1)} %reshape.195, bf16[24,4,16,32,32]{4,3,2,1,0:T(8,128)(2,1)} %reshape.207), kind=kOutput, calls=%fused_computation.73 | convolution fusion | flops 100663296 | bytes 6422528 | tf_op jit(solution)/shard_map/bhwgc,bhwgo->cgo/dot_general | solution.py:153
  1385.7 55.3 %fusion.35 = f32[32,32,32,1,1]{2,1,4,3,0:T(8,128)} fusion(bf16[24,4,16,32,32]{4,3,2,1,0:T(8,128)(2,1)} %reshape.196, bf16[24,4,16,32,32]{4,3,2,1,0:T(8,128)(2,1)} %reshape.207), kind=kOutput, calls=%fused_computation.69 | convolution fusion | flops 100663296 | bytes 6422528 | tf_op jit(solution)/shard_map/bhwgc,bhwgo->cgo/dot_general | solution.py:153
  1441.0 55.3 %fusion.31 = f32[32,32,32,1,1]{2,1,4,3,0:T(8,128)} fusion(bf16[24,4,16,32,32]{4,3,2,1,0:T(8,128)(2,1)} %reshape.197, bf16[24,4,16,32,32]{4,3,2,1,0:T(8,128)(2,1)} %reshape.207), kind=kOutput, calls=%fused_computation.65 | convolution fusion | flops 100663296 | bytes 6422528 | tf_op jit(solution)/shard_map/bhwgc,bhwgo->cgo/dot_general | solution.py:153
  1496.3 55.3 %fusion.27 = f32[32,32,32,1,1]{2,1,4,3,0:T(8,128)} fusion(bf16[24,4,16,32,32]{4,3,2,1,0:T(8,128)(2,1)} %reshape.198, bf16[24,4,16,32,32]{4,3,2,1,0:T(8,128)(2,1)} %reshape.207), kind=kOutput, calls=%fused_computation.61 | convolution fusion | flops 100663296 | bytes 6422528 | tf_op jit(solution)/shard_map/bhwgc,bhwgo->cgo/dot_general | solution.py:153
  1551.7 55.4 %fusion.23 = f32[32,32,32,1,1]{2,1,4,3,0:T(8,128)} fusion(bf16[24,4,16,32,32]{4,3,2,1,0:T(8,128)(2,1)} %reshape.199, bf16[24,4,16,32,32]{4,3,2,1,0:T(8,128)(2,1)} %reshape.207), kind=kOutput, calls=%fused_computation.57 | convolution fusion | flops 100663296 | bytes 6422528 | tf_op jit(solution)/shard_map/bhwgc,bhwgo->cgo/dot_general | solution.py:153
  1607.0 55.3 %fusion.19 = f32[32,32,32,1,1]{2,1,4,3,0:T(8,128)} fusion(bf16[24,4,16,32,32]{4,3,2,1,0:T(8,128)(2,1)} %reshape.200, bf16[24,4,16,32,32]{4,3,2,1,0:T(8,128)(2,1)} %reshape.207), kind=kOutput, calls=%fused_computation.53 | convolution fusion | flops 100663296 | bytes 6422528 | tf_op jit(solution)/shard_map/bhwgc,bhwgo->cgo/dot_general | solution.py:153
  1662.3 55.3 %fusion.15 = f32[32,32,32,1,1]{2,1,4,3,0:T(8,128)} fusion(bf16[24,4,16,32,32]{4,3,2,1,0:T(8,128)(2,1)} %reshape.201, bf16[24,4,16,32,32]{4,3,2,1,0:T(8,128)(2,1)} %reshape.207), kind=kOutput, calls=%fused_computation.49 | convolution fusion | flops 100663296 | bytes 6422528 | tf_op jit(solution)/shard_map/bhwgc,bhwgo->cgo/dot_general | solution.py:153
  1717.7 55.3 %fusion.11 = f32[32,32,32,1,1]{2,1,4,3,0:T(8,128)} fusion(bf16[24,4,16,32,32]{4,3,2,1,0:T(8,128)(2,1)} %reshape.202, bf16[24,4,16,32,32]{4,3,2,1,0:T(8,128)(2,1)} %reshape.207), kind=kOutput, calls=%fused_computation.45 | convolution fusion | flops 100663296 | bytes 6422528 | tf_op jit(solution)/shard_map/bhwgc,bhwgo->cgo/dot_general | solution.py:153
  1773.0 55.7 %fusion.7 = f32[32,32,32,1,1]{2,1,4,3,0:T(8,128)} fusion(bf16[24,4,16,32,32]{4,3,2,1,0:T(8,128)(2,1)} %reshape.203, bf16[24,4,16,32,32]{4,3,2,1,0:T(8,128)(2,1)} %reshape.207), kind=kOutput, calls=%fused_computation.41 | convolution fusion | flops 100663296 | bytes 6422528 | tf_op jit(solution)/shard_map/bhwgc,bhwgo->cgo/dot_general | solution.py:153
  2074.8 24.9 copy.239
  2120.0 24.9 copy.242
  2209.7 25.0 copy.249
  2299.4 25.2 copy.256
  2626.1 25.1 copy.266
  2675.1 38.7 %psum.47 = f32[2048]{0:T(1024)S(1)} all-reduce(f32[2048]{0:T(1024)S(1)} %pad_maximum_fusion.9), channel_id=1, replica_groups=mesh['batch'=8,'height'=4] {'batch','height'}, use_global_device_ids=true, to_apply=%region_20.21 | all-reduce | flops 2048 | bytes 16384 | tf_op jit(solution)/shard_map/psum | solution.py:187
  2783.6 361.1 %all-reduce.15 = bf16[5537792]{0:T(1024)(128)(2,1)} all-reduce(f32[5537792]{0:T(1024)} %pad_maximum_fusion.1), channel_id=2, replica_groups=mesh['batch'=8,'height'=4] {'batch','height'}, use_global_device_ids=true, to_apply=%region_21.22.clone | all-reduce | flops 5537792 | bytes 33226752
  (253 shorter events, 1468.8 us)
Async XLA Ops:
  7.2 3234.4 %all-gather.2.cloned.1.call-start = ((), (), s32[]{:S(2)}) async-start(), calls=%async_computation | async-start | bytes 11421696 | tf_op jit(solution)/shard_map/all_gather | solution.py:215
  8.8 63.2 %copy-start.31 = (f32[1024]{0:T(1024)S(1)}, f32[1024]{0:T(1024)}, u32[]{:S(2)}) copy-start(f32[1024]{0:T(1024)} %param.16) | copy-start | bytes 12292
  8.8 63.8 %copy-start.36 = (f32[1024]{0:T(1024)S(1)}, f32[1024]{0:T(1024)}, u32[]{:S(2)}) copy-start(f32[1024]{0:T(1024)} %param.17) | copy-start | bytes 12292
  72.6 73.9 %copy-start.25 = (bf16[3,3,32,1024]{3,2,1,0:T(8,128)(2,1)S(1)}, bf16[3,3,32,1024]{3,2,1,0:T(8,128)(2,1)}, u32[]{:S(2)}) copy-start(bf16[3,3,32,1024]{3,2,1,0:T(8,128)(2,1)} %param.18) | copy-start | bytes 1769476
  90.7 76.7 %collective-permute-start = (bf16[24,32,1024]{2,1,0:T(8,128)(2,1)}, bf16[24,32,1024]{2,1,0:T(8,128)(2,1)}, u32[]{:S(2)}, u32[]{:S(2)}) collective-permute-start(bf16[24,32,1024]{2,1,0:T(8,128)(2,1)} %slice_bitcast_fusion), channel_id=1, source_target_pairs={{0,1},{1,2},{2,3},{4,5},{5,6},{6,7},{8,9},{9,10},{10,11},{12,13},{... | collective-permute-start | bytes 4718600 | tf_op jit(solution)/shard_map/ppermute | solution.py:20
  147.4 637.8 %copy-start.6 = (bf16[32,32,32]{2,1,0:T(8,128)(2,1)}, bf16[32,32,32]{2,1,0:T(8,128)(2,1)S(1)}, u32[]{:S(2)}) copy-start(bf16[32,32,32]{2,1,0:T(8,128)(2,1)S(1)} %reshape_squeeze.43) | copy-start | bytes 196612
  147.6 657.7 %copy-start.14 = (bf16[32,32,32]{2,1,0:T(8,128)(2,1)}, bf16[32,32,32]{2,1,0:T(8,128)(2,1)S(1)}, u32[]{:S(2)}) copy-start(bf16[32,32,32]{2,1,0:T(8,128)(2,1)S(1)} %reshape_squeeze.42) | copy-start | bytes 196612
  147.8 677.7 %copy-start.8 = (bf16[32,32,32]{2,1,0:T(8,128)(2,1)}, bf16[32,32,32]{2,1,0:T(8,128)(2,1)S(1)}, u32[]{:S(2)}) copy-start(bf16[32,32,32]{2,1,0:T(8,128)(2,1)S(1)} %reshape_squeeze.41) | copy-start | bytes 196612
  148.0 697.6 %copy-start.10 = (bf16[32,32,32]{2,1,0:T(8,128)(2,1)}, bf16[32,32,32]{2,1,0:T(8,128)(2,1)S(1)}, u32[]{:S(2)}) copy-start(bf16[32,32,32]{2,1,0:T(8,128)(2,1)S(1)} %reshape_squeeze.40) | copy-start | bytes 196612
  149.1 716.8 %copy-start.12 = (bf16[32,32,32]{2,1,0:T(8,128)(2,1)}, bf16[32,32,32]{2,1,0:T(8,128)(2,1)S(1)}, u32[]{:S(2)}) copy-start(bf16[32,32,32]{2,1,0:T(8,128)(2,1)S(1)} %reshape_squeeze.39) | copy-start | bytes 196612
  865.9 20.2 copy-start.18
  886.0 20.6 copy-start.16
  906.6 20.1 copy-start.22
  926.7 20.3 copy-start.20
  1131.7 55.1 %copy-start.33 = (f32[2048]{0:T(1024)S(1)}, f32[2048]{0:T(1024)}, u32[]{:S(2)}) copy-start(f32[2048]{0:T(1024)} %param.25) | copy-start | bytes 24580
  1131.8 55.1 %copy-start.34 = (f32[2048]{0:T(1024)S(1)}, f32[2048]{0:T(1024)}, u32[]{:S(2)}) copy-start(f32[2048]{0:T(1024)} %param.22) | copy-start | bytes 24580
  1131.8 55.1 %copy-start.39 = (f32[2048]{0:T(1024)S(1)}, f32[2048]{0:T(1024)}, u32[]{:S(2)}) copy-start(f32[2048]{0:T(1024)} %param.26) | copy-start | bytes 24580
  1131.8 55.1 %copy-start.40 = (f32[2048]{0:T(1024)S(1)}, f32[2048]{0:T(1024)}, u32[]{:S(2)}) copy-start(f32[2048]{0:T(1024)} %param.23) | copy-start | bytes 24580
  1717.7 111.0 %slice-start.6 = ((s8[6291456]{0:T(1024)(128)(4,1)}), s8[4194304]{0:T(1024)(128)(4,1)S(1)}, s32[]{:S(2)}) async-start(s8[6291456]{0:T(1024)(128)(4,1)} %bitcast.239), calls=%async_computation.7 | async-start | bytes 8388608
  1773.0 55.7 %slice-start.7 = ((s8[6291456]{0:T(1024)(128)(4,1)}), s8[2097152]{0:T(1024)(128)(4,1)S(1)}, s32[]{:S(2)}) async-start(s8[6291456]{0:T(1024)(128)(4,1)} %bitcast.239), calls=%async_computation.8 | async-start | bytes 4194304
  2567.6 37.5 %collective-permute-start.1 = (bf16[24,32,1024]{2,0,1:T(8,128)(2,1)}, bf16[24,32,1024]{2,0,1:T(8,128)(2,1)}, u32[]{:S(2)}, u32[]{:S(2)}) collective-permute-start(bf16[24,32,1024]{2,0,1:T(8,128)(2,1)} %fusion.43), channel_id=1, source_target_pairs={{1,0},{2,1},{3,2},{5,4},{6,5},{7,6},{9,8},{10,9},{11,10},{13,12},{... | collective-permute-start | bytes 4718600 | tf_op jit(solution)/shard_map/ppermute | solution.py:20
  2605.1 46.1 %slice-start = ((s8[25165824]{0:T(1024)(128)(4,1)}), s8[4194304]{0:T(1024)(128)(4,1)S(1)}, s32[]{:S(2)}) async-start(s8[25165824]{0:T(1024)(128)(4,1)} %bitcast.224), calls=%async_computation.1 | async-start | bytes 8388608
  2605.1 46.1 %slice-start.1 = ((s8[25165824]{0:T(1024)(128)(4,1)}), s8[4194304]{0:T(1024)(128)(4,1)S(1)}, s32[]{:S(2)}) async-start(s8[25165824]{0:T(1024)(128)(4,1)} %bitcast.224), calls=%async_computation.2 | async-start | bytes 8388608
  2605.1 46.1 %slice-start.2 = ((s8[25165824]{0:T(1024)(128)(4,1)}), s8[4194304]{0:T(1024)(128)(4,1)S(1)}, s32[]{:S(2)}) async-start(s8[25165824]{0:T(1024)(128)(4,1)} %bitcast.224), calls=%async_computation.3 | async-start | bytes 8388608
  2605.1 46.1 %slice-start.3 = ((s8[25165824]{0:T(1024)(128)(4,1)}), s8[4194304]{0:T(1024)(128)(4,1)S(1)}, s32[]{:S(2)}) async-start(s8[25165824]{0:T(1024)(128)(4,1)} %bitcast.224), calls=%async_computation.4 | async-start | bytes 8388608
  2626.1 25.2 slice-start.4
  2626.1 25.2 slice-start.5
  2626.1 25.2 copy-start.28
  2626.1 25.2 copy-start.30
  2626.1 25.2 copy-start.32
  2626.1 25.2 copy-start.37
  2651.3 63.1 %copy-start.38 = (f32[1024]{0:T(1024)S(1)}, f32[1024]{0:T(1024)}, u32[]{:S(2)}) copy-start(f32[1024]{0:T(1024)} %get-tuple-element.70) | copy-start | bytes 12292
  (25 other events, 358.1 us)
Sparse Core Ops, SparseCore 0:
  3146.5 87.5 all-gather.1
where the time goes:
time: 3320 us; the launch traced here: 3290 us
  local copies, waits for them, and re-layouts  1350 us (41%)
  matrix products  960 us (29%)
  blocking collectives  602 us (18%)
  other arithmetic  342 us (10%)
    dot_general x9, matrix products, per_device(): jnp.einsum('bhwgc,bhwgo->cgo', window, mid_grad, preferred_element_type=j...  486 us
    slice x9, local copies, waits for them, and re-layouts, per_device(): window = padded[:, tap_row:tap_row + rows_in:2, tap_col:tap_col + W_IN:2, :]  459 us
    unnamed x1, blocking collectives  361 us
    transpose x8, local copies, waits for them, and re-layouts, per_device(): jnp.einsum('bhwgo,cgo->bhwgc', mid_grad, kernel, preferred_element_type=j...  200 us
    dot_general x9, matrix products, per_device(): jnp.einsum('bhwgc,cgo->bhwgo', window, kernel, preferred_element_type=jnp...  182 us
    reshape x8, local copies, waits for them, and re-layouts, per_device(): tap_grad = jnp.einsum('bhwgo,cgo->bhwgc', mid_grad, kernel, preferred_ele...  160 us
    dot_general x9, matrix products, per_device(): jnp.einsum('bhwgo,cgo->bhwgc', mid_grad, kernel, preferred_element_type=j...  160 us
    reshape x9, local copies, waits for them, and re-layouts, per_device(): window = window.reshape(img_count, rows_out, cols_out, GROUPS, GW)  141 us
  transfers between devices with their start and end apart: 3, of which 1 were waited for; matrix products, arithmetic and copies ran while one was open for 6% of the time, Pallas kernels for 0%

commit v1 on v0

v1 whole, which is shorter than its diff:
```python
import functools

import jax
import jax.numpy as jnp
from jax import lax
from jax.experimental import pallas as pl
from jax.experimental.pallas import tpu as pltpu
from jax.sharding import PartitionSpec as P

EPSILON = 1e-05
LANES = 128
CHUNK = 256
BF16 = jnp.bfloat16
F32 = jnp.float32
MIB = 1 << 20


def dot(a, b):
    return jnp.dot(a, b, preferred_element_type=F32)


def dot_nt(a, b):
    return lax.dot_general(a, b, (((1,), (1,)), ((), ())), preferred_element_type=F32)


def dot_tn(a, b):
    return lax.dot_general(a, b, (((0,), (0,)), ((), ())), preferred_element_type=F32)


def fold(values):
    rows, cols = values.shape
    return jnp.sum(values.reshape(rows // 8, 8, cols), axis=0)


def put_row(ref, first, row):
    for k in range(row.shape[1] // LANES):
        ref[first + k : first + k + 1, :] = row[:, k * LANES : (k + 1) * LANES]


def get_row(values, first, width):
    count = width // LANES
    return jnp.concatenate([values[first + k : first + k + 1, :] for k in range(count)], axis=1)


def sums_out(ref, *partials):
    first = 0
    for part in partials:
        row = jnp.sum(part, axis=0, keepdims=True)
        put_row(ref, first, row)
        first += row.shape[1] // LANES


def whole(shape):
    return pl.BlockSpec(shape, lambda *_: (0,) * len(shape), pipeline_mode=pl.Buffered(1))


def rows_spec(rows, cols):
    return pl.BlockSpec((rows, cols), lambda i: (i, 0))


def call(body, name, grid, in_specs, out_specs, out_shape, scratch=(), flops=0, moved=0, vmem=56):
    return pl.pallas_call(
        body,
        name=name,
        grid=grid,
        in_specs=in_specs,
        out_specs=out_specs,
        out_shape=out_shape,
        scratch_shapes=list(scratch),
        compiler_params=pltpu.CompilerParams(vmem_limit_bytes=vmem * MIB),
        cost_estimate=pl.CostEstimate(flops=flops, bytes_accessed=moved, transcendentals=0),
    )


def shape(dims, kind=F32):
    return jax.ShapeDtypeStruct(dims, kind)


def exchange_body(epilogue, outs, in_ref, *rest):
    n_par = len(rest) - outs - 6
    params = rest[:n_par]
    out_refs = rest[n_par : n_par + outs]
    got_b, got_h, send_b, recv_b, send_h, recv_h = rest[n_par + outs :]
    size_b, size_h = got_b.shape[0], got_h.shape[0]
    me_b, me_h = lax.axis_index("batch"), lax.axis_index("height")
    barrier = pltpu.get_barrier_semaphore()
    peers = [(lax.rem(me_b + k, size_b), me_h) for k in range(1, size_b)]
    peers_h = [(me_b, lax.rem(me_h + k, size_h)) for k in range(1, size_h)]
    for peer in peers + peers_h:
        pl.semaphore_signal(barrier, inc=1, device_id=peer, device_id_type=pl.DeviceIdType.MESH)
    pl.semaphore_wait(barrier, len(peers) + len(peers_h))

    def spread(src, got, me, targets, size, send, recv):
        copies = []
        for k, peer in enumerate(targets):
            copy = pltpu.make_async_remote_copy(
                src_ref=src,
                dst_ref=got.at[me],
                send_sem=send.at[k],
                recv_sem=recv.at[me],
                device_id=peer,
                device_id_type=pl.DeviceIdType.MESH,
            )
            copy.start()
            copies.append(copy)
        for k, peer in enumerate(targets):
            other = lax.rem(me + (size - 1 - k), size)
            pltpu.make_async_remote_copy(
                src_ref=src,
                dst_ref=got.at[other],
                send_sem=send.at[k],
                recv_sem=recv.at[other],
                device_id=peer,
                device_id_type=pl.DeviceIdType.MESH,
            ).wait_recv()
        total = got[0]
        for k in range(1, size):
            total = total + got[k]
        return total, copies

    got_b[me_b] = in_ref[...]
    part, copies_b = spread(in_ref, got_b, me_b, peers, size_b, send_b, recv_b)
    got_h[me_h] = part
    total, copies_h = spread(got_h.at[me_h], got_h, me_h, peers_h, size_h, send_h, recv_h)
    epilogue(total, params, out_refs)
    for copy in copies_b + copies_h:
        copy.wait_send()


def exchange(sums, params, epilogue, out_shape, ident):
    rows = sums.shape[0]
    size_b, size_h = lax.axis_size("batch"), lax.axis_size("height")
    vmem = pl.BlockSpec(memory_space=pltpu.VMEM)
    return pl.pallas_call(
        functools.partial(exchange_body, epilogue, len(out_shape)),
        name="exchange_%d" % ident,
        in_specs=[vmem] * (1 + len(params)),
        out_specs=[vmem] * len(out_shape),
        out_shape=out_shape,
        scratch_shapes=[
            pltpu.VMEM((size_b, rows, LANES), F32),
            pltpu.VMEM((size_h, rows, LANES), F32),
            pltpu.SemaphoreType.DMA((size_b - 1,)),
            pltpu.SemaphoreType.DMA((size_b,)),
            pltpu.SemaphoreType.DMA((size_h - 1,)),
            pltpu.SemaphoreType.DMA((size_h,)),
        ],
        compiler_params=pltpu.CompilerParams(collective_id=ident, has_side_effects=True),
        cost_estimate=pl.CostEstimate(flops=1000, bytes_accessed=100000, transcendentals=0),
    )(sums, *params)


def norm_terms(total, first, width, cells):
    average = get_row(total, first, width) * (1.0 / cells)
    meansq = get_row(total, first + width // LANES, width) * (1.0 / cells)
    inverse = lax.rsqrt(meansq - average * average + EPSILON)
    return inverse, -average * inverse


def fill(ref, rows):
    for k, row in enumerate(rows):
        ref[k : k + 1, :] = row
    ref[len(rows) :, :] = jnp.zeros((8 - len(rows), ref.shape[1]), F32)


def act_rows(inverse, offset, gain, shift):
    return [
        inverse,
        offset,
        0.5 * gain,
        0.5 * shift,
        0.5 * gain * inverse,
        0.5 * (shift + gain * offset),
    ]


def first_totals(cells_in, cells_out, width, wide, total, params, outs):
    gain, shift = params[0][0:1, :], params[0][1:2, :]
    fill(outs[0], act_rows(*norm_terms(total, 0, width, cells_in), gain, shift))
    fill(outs[1], list(norm_terms(total, 2 * width // LANES, wide, cells_out)))


def mid_totals(cells_out, width, total, params, outs):
    gain, shift = params[0][2:3, :], params[0][3:4, :]
    fill(outs[0], act_rows(*norm_terms(total, 0, width, cells_out), gain, shift))


def last_totals(cells_out, wide, total, params, outs):
    wides, side = params
    inverse, offset = norm_terms(total, 0, wide, cells_out)
    fill(
        outs[0],
        [
            inverse,
            offset,
            side[0:1, :],
            side[1:2, :],
            0.5 * wides[0:1, :],
            0.5 * wides[2:3, :],
            0.5 * (wides[1:2, :] + wides[3:4, :]),
        ],
    )


def back_rows(gain, inverse, total_up, cross, cells):
    scale = gain * inverse
    return [0.5 * scale, -scale * total_up * (1.0 / cells), -scale * cross * (1.0 / cells)]


def out_totals(cells_out, wide, total, params, outs):
    coef = params[0]
    step = wide // LANES
    total_up, last_cross, side_cross = [
        0.5 * get_row(total, k * step, wide) for k in range(3)
    ]
    fill(
        outs[0],
        back_rows(2.0 * coef[4:5, :], coef[0:1, :], total_up, last_cross, cells_out)
        + back_rows(2.0 * coef[5:6, :], coef[2:3, :], total_up, side_cross, cells_out),
    )
    fill(outs[1], [total_up, last_cross, side_cross])


def inner_totals(cells, width, total, params, outs):
    coef = params[0]
    total_up = 0.5 * get_row(total, 0, width)
    cross = 0.5 * get_row(total, width // LANES, width)
    fill(outs[0], back_rows(2.0 * coef[2:3, :], coef[0:1, :], total_up, cross, cells))
    fill(outs[1], [total_up, cross])


def half_silu(half):
    return half + half * jnp.tanh(half)


def slope_twice(half, th):
    return (1.0 + th) * (1.0 + half * (1.0 - th))


def first_body(per, px, q, img, perm, w1, ws, xp, pre, side, stat, acc, acc_s):
    step = pl.program_id(0)
    mid, wide = w1.shape[1], ws.shape[1]

    @pl.when(step == 0)
    def _():
        acc[...] = jnp.zeros_like(acc)
        acc_s[...] = jnp.zeros_like(acc_s)

    for k in range(per):
        flat = img[k].reshape(px, img.shape[3])
        moved = dot(perm[...], flat).astype(BF16)
        xp[k * px : (k + 1) * px, :] = moved
        for c in range(0, mid, CHUNK):
            cols = slice(c, c + CHUNK)
            part = dot(moved, w1[:, cols])
            pre[k * px : (k + 1) * px, cols] = part
            acc[0:8, cols] += fold(part)
            acc[8:16, cols] += fold(part * part)
    even = jnp.concatenate([xp[k * px : k * px + q, :] for k in range(per)], axis=0)
    for c in range(0, wide, CHUNK):
        cols = slice(c, c + CHUNK)
        part = dot(even, ws[:, cols])
        side[:, cols] = part
        acc_s[0:8, cols] += fold(part)
        acc_s[8:16, cols] += fold(part * part)

    @pl.when(step == pl.num_programs(0) - 1)
    def _():
        sums_out(stat, acc[0:8, :], acc[8:16, :], acc_s[0:8, :], acc_s[8:16, :])


def conv_body(per, px, q, pre, halo, flag, w1, perm, coef, wbd, mid, stat, a00, a01, a10, a11, acc):
    step = pl.program_id(0)
    width = w1.shape[1]

    @pl.when(step == 0)
    def _():
        acc[...] = jnp.zeros_like(acc)

    scale, offset = coef[4:5, :], coef[5:6, :]
    flat = halo[...].reshape(per * 32, halo.shape[2])
    rim = dot(dot(perm[...], flat).astype(BF16), w1[...])
    rim = (half_silu(rim * scale + offset) * flag[0]).astype(BF16)
    rim = rim.reshape(per, 2, 16, width)
    a10[:, 0:16, :] = rim[:, 0]
    a11[:, 0:16, :] = rim[:, 1]
    for plane, ref, top in ((0, a00, 0), (1, a01, 0), (2, a10, 16), (3, a11, 16)):
        half = pre[:, plane] * scale[None] + offset[None]
        ref[:, top : top + q, :] = half_silu(half).astype(BF16)
    rows = per * q
    first_col = lax.broadcasted_iota(jnp.int32, (rows, CHUNK), 0) % 16 == 0
    for c in range(0, width, CHUNK):
        cols = slice(c, c + CHUNK)

        def tap(ref, top, row, col):
            return dot(ref[:, top : top + q, cols].reshape(rows, CHUNK), wbd[row * 3 + col, :, cols])

        straight = (
            tap(a00, 0, 1, 1)
            + tap(a01, 0, 1, 2)
            + tap(a10, 16, 2, 1)
            + tap(a11, 16, 2, 2)
            + tap(a10, 0, 0, 1)
            + tap(a11, 0, 0, 2)
        )
        moved = tap(a01, 0, 1, 0) + tap(a11, 16, 2, 0) + tap(a11, 0, 0, 0)
        part = straight + jnp.where(first_col, 0.0, pltpu.roll(moved, 1, 0))
        mid[:, cols] = part
        acc[0:8, cols] += fold(part)
        acc[8:16, cols] += fold(part * part)

    @pl.when(step == pl.num_programs(0) - 1)
    def _():
        sums_out(stat, acc[0:8, :], acc[8:16, :])


def last_body(mid, coef, w, act, pre, stat, acc):
    step = pl.program_id(0)

    @pl.when(step == 0)
    def _():
        acc[...] = jnp.zeros_like(acc)

    half = mid[...] * coef[4:5, :] + coef[5:6, :]
    act[...] = half_silu(half).astype(BF16)
    for c in range(0, w.shape[1], CHUNK):
        cols = slice(c, c + CHUNK)
        part = dot(act[...], w[:, cols])
        pre[:, cols] = part
        acc[0:8, cols] += fold(part)
        acc[8:16, cols] += fold(part * part)

    @pl.when(step == pl.num_programs(0) - 1)
    def _():
        sums_out(stat, acc[0:8, :], acc[8:16, :])


def out_parts(last, side, cot, coef, cols):
    last_normed = last[:, cols] * coef[0:1, cols] + coef[1:2, cols]
    side_normed = side[:, cols] * coef[2:3, cols] + coef[3:4, cols]
    half = last_normed * coef[4:5, cols] + side_normed * coef[5:6, cols] + coef[6:7, cols]
    th = jnp.tanh(half)
    up = cot[:, cols].astype(F32) * slope_twice(half, th)
    return last_normed, side_normed, half, th, up


def out_body(last, side, cot, coef, out, stat, acc):
    step = pl.program_id(0)

    @pl.when(step == 0)
    def _():
        acc[...] = jnp.zeros_like(acc)

    for c in range(0, last.shape[1], CHUNK):
        cols = slice(c, c + CHUNK)
        last_normed, side_normed, half, th, up = out_parts(last, side, cot, coef, cols)
        out[:, cols] = (half + half * th).astype(BF16)
        acc[0:8, cols] += fold(up)
        acc[8:16, cols] += fold(up * last_normed)
        acc[16:24, cols] += fold(up * side_normed)

    @pl.when(step == pl.num_programs(0) - 1)
    def _():
        sums_out(stat, acc[0:8, :], acc[8:16, :], acc[16:24, :])


def tail_body(per, q, last, side, cot, coef, back, act, even, lg, sg, g_last, g_side, acc_l, acc_s):
    step = pl.program_id(0)

    @pl.when(step == 0)
    def _():
        acc_l[...] = jnp.zeros_like(acc_l)
        acc_s[...] = jnp.zeros_like(acc_s)

    flat = even[...].reshape(per * q, even.shape[3])
    for c in range(0, last.shape[1], CHUNK):
        cols = slice(c, c + CHUNK)
        last_normed, side_normed, _, _, up = out_parts(last, side, cot, coef, cols)
        down = (up * back[0:1, cols] + back[1:2, cols] + last_normed * back[2:3, cols]).astype(BF16)
        lg[:, cols] = down
        acc_l[:, cols] += dot_tn(act[...], down)
        down = (up * back[3:4, cols] + back[4:5, cols] + side_normed * back[5:6, cols]).astype(BF16)
        sg[:, cols] = down
        acc_s[:, cols] += dot_tn(flat, down)

    @pl.when(step == pl.num_programs(0) - 1)
    def _():
        g_last[...] = acc_l[...].astype(BF16)
        g_side[...] = acc_s[...].astype(BF16)


def mid_back_body(lg, sg, wl, ws, mid, coef, up, side_back, stat, acc):
    step = pl.program_id(0)

    @pl.when(step == 0)
    def _():
        acc[...] = jnp.zeros_like(acc)

    for c in range(0, mid.shape[1], CHUNK):
        cols = slice(c, c + CHUNK)
        part = dot_nt(lg[...], wl[cols, :])
        normed = mid[:, cols] * coef[0:1, cols] + coef[1:2, cols]
        half = normed * coef[2:3, cols] + coef[3:4, cols]
        part = part * slope_twice(half, jnp.tanh(half))
        up[:, cols] = part
        acc[0:8, cols] += fold(part)
        acc[8:16, cols] += fold(part * normed)
        side_back[:, cols] = dot_nt(sg[...], ws[cols, :])

    @pl.when(step == pl.num_programs(0) - 1)
    def _():
        sums_out(stat, acc[0:8, :], acc[8:16, :])


def conv_back_body(
    per, px, q, mup, mid, halo, pre, coef2, back, coef, wbd, up, g_mid, stat, mg, mgs, acc, acc_g
):
    step = pl.program_id(0)
    width = mid.shape[1]
    rows = per * q

    @pl.when(step == 0)
    def _():
        acc[...] = jnp.zeros_like(acc)
        acc_g[...] = jnp.zeros_like(acc_g)

    ext = q + 16
    last_col = lax.broadcasted_iota(jnp.int32, (rows, CHUNK), 0) % 16 == 15
    last_rim = lax.broadcasted_iota(jnp.int32, (per * 16, CHUNK), 0) % 16 == 15
    for c in range(0, width, CHUNK):
        cols = slice(c, c + CHUNK)
        normed = mid[:, cols] * coef2[0:1, cols] + coef2[1:2, cols]
        grad = (mup[:, cols] * back[0:1, cols] + back[1:2, cols] + normed * back[2:3, cols]).astype(BF16)
        mg[:, 0:q, cols] = grad.reshape(per, q, CHUNK)
        grad = pltpu.roll(grad.astype(F32), rows - 1, 0)
        mgs[:, 0:q, cols] = jnp.where(last_col, 0.0, grad).astype(BF16).reshape(per, q, CHUNK)
        rim = halo[:, :, cols]
        mg[:, q:ext, cols] = rim
        rim = pltpu.roll(rim.reshape(per * 16, CHUNK).astype(F32), per * 16 - 1, 0)
        mgs[:, q:ext, cols] = jnp.where(last_rim, 0.0, rim).astype(BF16).reshape(per, 16, CHUNK)
        views = [ref[:, top : top + q, cols].reshape(rows, CHUNK) for top in (0, 16) for ref in (mg, mgs)]
        plans = (
            (0, ((1, 1, 0),)),
            (1, ((1, 2, 0), (1, 0, 1))),
            (2, ((2, 1, 0), (0, 1, 2))),
            (3, ((2, 2, 0), (2, 0, 1), (0, 2, 2), (0, 0, 3))),
        )
        for plane, taps in plans:
            total = None
            for row, col, view in taps:
                part = dot_nt(views[view], wbd[row * 3 + col, :, cols])
                total = part if total is None else total + part
            normed = pre[:, plane, :, cols].reshape(rows, CHUNK) * coef[0:1, cols] + coef[1:2, cols]
            half = normed * coef[2:3, cols] + coef[3:4, cols]
            th = jnp.tanh(half)
            act = (half + half * th).astype(BF16)
            total = total * slope_twice(half, th)
            up[:, plane, :, cols] = total.reshape(per, q, CHUNK)
            acc[0:8, cols] += fold(total)
            acc[8:16, cols] += fold(total * normed)
            for row, col, view in taps:
                acc_g[row * 3 + col, :, cols] += dot_tn(act, views[view])

    @pl.when(step == pl.num_programs(0) - 1)
    def _():
        sums_out(stat, acc[0:8, :], acc[8:16, :])
        group = (lax.broadcasted_iota(jnp.int32, (32, width), 1) % CHUNK) // 32
        for tap in range(9):
            total = jnp.zeros((32, width), F32)
            for g in range(CHUNK // 32):
                total = total + jnp.where(group == g, acc_g[tap, g * 32 : (g + 1) * 32, :], 0.0)
            g_mid[tap] = total.astype(BF16)


def first_back_body(up, pre, coef, back, xp, fg, g_first, acc):
    step = pl.program_id(0)

    @pl.when(step == 0)
    def _():
        acc[...] = jnp.zeros_like(acc)

    for c in range(0, up.shape[1], CHUNK):
        cols = slice(c, c + CHUNK)
        normed = pre[:, cols] * coef[0:1, cols] + coef[1:2, cols]
        down = (up[:, cols] * back[0:1, cols] + back[1:2, cols] + normed * back[2:3, cols]).astype(BF16)
        fg[:, cols] = down
        acc[:, cols] += dot_tn(xp[...], down)

    @pl.when(step == pl.num_programs(0) - 1)
    def _():
        g_first[...] = acc[...].astype(BF16)


def image_back_body(per, px, q, fg, w1, side_back, perm, out):
    cin = w1.shape[0]
    for k in range(per):
        for c in range(0, cin, CHUNK):
            cols = slice(c, c + CHUNK)
            part = dot_nt(fg[k * px : (k + 1) * px, :], w1[cols, :])
            even = part[0:q] + side_back[k * q : (k + 1) * q, cols]
            part = jnp.concatenate([even, part[q:]], axis=0).astype(BF16)
            part = dot_tn(perm[...], part).astype(BF16)
            out[k, :, :, cols] = part.reshape(out.shape[1], out.shape[2], CHUNK)


def flip(axis, bit):
    return [(i, i ^ (1 << bit)) for i in range(lax.axis_size(axis))]


def halve(part, axis, bit):
    mine = (lax.axis_index(axis) >> bit) & 1
    half = part.shape[0] // 2
    send = lax.dynamic_slice_in_dim(part, (1 - mine) * half, half, 0)
    got = lax.ppermute(send, axis, flip(axis, bit))
    keep = lax.dynamic_slice_in_dim(part, mine * half, half, 0)
    return (keep.astype(F32) + got.astype(F32)).astype(BF16)


def double(part, axis, bit):
    mine = (lax.axis_index(axis) >> bit) & 1
    got = lax.ppermute(part, axis, flip(axis, bit))
    return jnp.concatenate([jnp.where(mine == 1, got, part), jnp.where(mine == 1, part, got)], axis=0)


def orders():
    bits_b = lax.axis_size("batch").bit_length() - 1
    bits_h = lax.axis_size("height").bit_length() - 1
    near = [("batch", 0)]
    across = [("batch", k) for k in range(1, bits_b)]
    half = len(across) // 2
    x_bits, y_bits = across[:half], across[half:]
    z_bits = [("height", k) for k in range(bits_h)]
    return [near + x_bits + y_bits + z_bits, near + y_bits + z_bits + x_bits, near + z_bits + x_bits + y_bits]


def sum_all(parts):
    totals = []
    for part, order in zip(parts, orders()):
        for axis, bit in order:
            part = halve(part, axis, bit)
        for axis, bit in reversed(order):
            part = double(part, axis, bit)
        totals.append(part)
    return totals


def split_sum(rows_2d):
    count = rows_2d.shape[0]
    unit = lax.axis_size("batch") * lax.axis_size("height") * 16
    cuts = [0]
    for k in range(3):
        cuts.append(min(count, cuts[-1] + -(-(count - cuts[-1]) // ((3 - k) * unit)) * unit))
    parts = [rows_2d[a:b] for a, b in zip(cuts, cuts[1:]) if b > a]
    return jnp.concatenate(sum_all(parts), axis=0)


def per_device(
    images,
    w_first,
    gain_first,
    shift_first,
    w_mid,
    gain_mid,
    shift_mid,
    w_last,
    gain_last,
    shift_last,
    w_side,
    gain_side,
    shift_side,
    cotangent,
):
    n, rows_in, cols_in, cin = images.shape
    mid = w_first.shape[1]
    wide = w_last.shape[1]
    gw = w_mid.shape[2]
    rows_out, cols_out = rows_in // 2, cols_in // 2
    px, q = rows_in * cols_in, rows_out * cols_out
    devices = lax.axis_size("batch") * lax.axis_size("height")
    cells_in = float(n * px * devices)
    cells_out = float(n * q * devices)
    size_h = lax.axis_size("height")
    per = 4
    steps = n // per
    rows = per * q

    halo_x = lax.ppermute(images[:, rows_in - 1], "height", [(i, i + 1) for i in range(size_h - 1)])

    narrow = jnp.stack([gain_first, shift_first, gain_mid, shift_mid] + [jnp.zeros_like(gain_mid)] * 4)
    wides = jnp.stack([gain_last, shift_last, gain_side, shift_side] + [jnp.zeros_like(gain_last)] * 4)
    flag = (lax.axis_index("height") > 0).astype(F32).reshape(1)
    tiled = jnp.tile(w_mid.reshape(9, 1, gw, mid), (1, CHUNK // gw, 1, 1))
    same = (
        lax.broadcasted_iota(jnp.int32, (CHUNK // gw, gw, mid), 0)
        == (lax.broadcasted_iota(jnp.int32, (CHUNK // gw, gw, mid), 2) % CHUNK) // gw
    )
    wbd = jnp.where(same[None], tiled, 0).reshape(9, CHUNK, mid).astype(BF16)

    place = lax.broadcasted_iota(jnp.int32, (px, px), 0)
    plane, i, j = place // q, (place % q) // cols_out, place % cols_out
    source = (2 * i + plane // 2) * cols_in + 2 * j + plane % 2
    perm = (source == lax.broadcasted_iota(jnp.int32, (px, px), 1)).astype(BF16)
    size_p = per * cols_in
    place = lax.broadcasted_iota(jnp.int32, (size_p, size_p), 0)
    source = (place // cols_in) * cols_in + 2 * (place % cols_out) + (place % cols_in) // cols_out
    perm_rim = (source == lax.broadcasted_iota(jnp.int32, (size_p, size_p), 1)).astype(BF16)

    xp, pre, side_pre, stat = call(
        functools.partial(first_body, per, px, q),
        "first_product",
        (steps,),
        [
            pl.BlockSpec((per, rows_in, cols_in, cin), lambda s: (s, 0, 0, 0)),
            whole((px, px)),
            whole((cin, mid)),
            whole((cin, wide)),
        ],
        [
            rows_spec(per * px, cin),
            rows_spec(per * px, mid),
            rows_spec(rows, wide),
            whole((2 * (mid + wide) // LANES, LANES)),
        ],
        [
            shape((n * px, cin), BF16),
            shape((n * px, mid)),
            shape((n * q, wide)),
            shape((2 * (mid + wide) // LANES, LANES)),
        ],
        [pltpu.VMEM((16, mid), F32), pltpu.VMEM((16, wide), F32)],
        flops=2 * n * (px * cin * (mid + px) + q * cin * wide),
        moved=n * px * cin * 8 + n * q * wide * 4 + cin * (mid + wide) * 2,
    )(images, perm, w_first, w_side)
    coef1, side_coef = exchange(
        stat,
        [narrow],
        functools.partial(first_totals, cells_in, cells_out, mid, wide),
        [shape((8, mid)), shape((8, wide))],
        0,
    )

    pre_planes = pre.reshape(n, 4, q, mid)
    planes_spec = pl.BlockSpec((per, 4, q, mid), lambda s: (s, 0, 0, 0))
    mid_pre, stat = call(
        functools.partial(conv_body, per, px, q),
        "grouped_conv",
        (steps,),
        [
            planes_spec,
            pl.BlockSpec((per, cols_in, cin), lambda s: (s, 0, 0)),
            pl.BlockSpec(memory_space=pltpu.SMEM),
            whole((cin, mid)),
            whole((size_p, size_p)),
            whole((8, mid)),
            whole((9, CHUNK, mid)),
        ],
        [rows_spec(rows, mid), whole((2 * mid // LANES, LANES))],
        [shape((n * q, mid)), shape((2 * mid // LANES, LANES))],
        [
            pltpu.VMEM((per, q, mid), BF16),
            pltpu.VMEM((per, q, mid), BF16),
            pltpu.VMEM((per, q + 16, mid), BF16),
            pltpu.VMEM((per, q + 16, mid), BF16),
            pltpu.VMEM((16, mid), F32),
        ],
        flops=2 * n * q * mid * CHUNK * 9 + 2 * n * cols_in * cin * mid,
        moved=n * px * mid * 4 + n * q * mid * 4,
    )(pre_planes, halo_x, flag, w_first, perm_rim, coef1, wbd)
    (coef2,) = exchange(
        stat, [narrow], functools.partial(mid_totals, cells_out, mid), [shape((8, mid))], 1
    )

    mid_act, last_pre, stat = call(
        last_body,
        "last_product",
        (steps,),
        [rows_spec(rows, mid), whole((8, mid)), whole((mid, wide))],
        [rows_spec(rows, mid), rows_spec(rows, wide), whole((2 * wide // LANES, LANES))],
        [shape((n * q, mid), BF16), shape((n * q, wide)), shape((2 * wide // LANES, LANES))],
        [pltpu.VMEM((16, wide), F32)],
        flops=2 * n * q * mid * wide,
        moved=n * q * (mid * 6 + wide * 4),
    )(mid_pre, coef2, w_last)
    (coef3,) = exchange(
        stat,
        [wides, side_coef],
        functools.partial(last_totals, cells_out, wide),
        [shape((8, wide))],
        2,
    )

    cot = cotangent.reshape(n * q, wide)
    output, stat = call(
        out_body,
        "output",
        (steps,),
        [rows_spec(rows, wide), rows_spec(rows, wide), rows_spec(rows, wide), whole((8, wide))],
        [rows_spec(rows, wide), whole((3 * wide // LANES, LANES))],
        [shape((n * q, wide), BF16), shape((3 * wide // LANES, LANES))],
        [pltpu.VMEM((24, wide), F32)],
        flops=30 * n * q * wide,
        moved=n * q * wide * 12,
    )(last_pre, side_pre, cot, coef3)
    coef4, wide_grads = exchange(
        stat,
        [coef3],
        functools.partial(out_totals, cells_out, wide),
        [shape((8, wide)), shape((8, wide))],
        3,
    )

    xp_planes = xp.reshape(n, 4, q, cin)
    last_grad, side_grad, g_last, g_side = call(
        functools.partial(tail_body, per, q),
        "last_gradients",
        (steps,),
        [
            rows_spec(rows, wide),
            rows_spec(rows, wide),
            rows_spec(rows, wide),
            whole((8, wide)),
            whole((8, wide)),
            rows_spec(rows, mid),
            pl.BlockSpec((per, 1, q, cin), lambda s: (s, 0, 0, 0)),
        ],
        [rows_spec(rows, wide), rows_spec(rows, wide), whole((mid, wide)), whole((cin, wide))],
        [
            shape((n * q, wide), BF16),
            shape((n * q, wide), BF16),
            shape((mid, wide), BF16),
            shape((cin, wide), BF16),
        ],
        [pltpu.VMEM((mid, wide), F32), pltpu.VMEM((cin, wide), F32)],
        flops=4 * n * q * mid * wide,
        moved=n * q * (wide * 14 + mid * 4) + (mid + cin) * wide * 2,
        vmem=60,
    )(last_pre, side_pre, cot, coef3, coef4, mid_act, xp_planes)
    half = wide // 2
    tail_sum = split_sum(
        jnp.concatenate([g_last[:, :half], g_last[:, half:], g_side[:, :half], g_side[:, half:]], axis=0)
    )
    g_last = jnp.concatenate([tail_sum[:mid], tail_sum[mid : 2 * mid]], axis=1).astype(F32)
    g_side = jnp.concatenate([tail_sum[2 * mid : 2 * mid + cin], tail_sum[2 * mid + cin :]], axis=1).astype(F32)

    mid_up, side_back, stat = call(
        mid_back_body,
        "mid_back",
        (steps,),
        [
            rows_spec(rows, wide),
            rows_spec(rows, wide),
            whole((mid, wide)),
            whole((cin, wide)),
            rows_spec(rows, mid),
            whole((8, mid)),
        ],
        [rows_spec(rows, mid), rows_spec(rows, cin), whole((2 * mid // LANES, LANES))],
        [shape((n * q, mid)), shape((n * q, cin)), shape((2 * mid // LANES, LANES))],
        [pltpu.VMEM((16, mid), F32)],
        flops=4 * n * q * mid * wide,
        moved=n * q * (wide * 4 + mid * 12) + (mid + cin) * wide * 2,
    )(last_grad, side_grad, w_last, w_side, mid_pre, coef2)
    coef5, mid_grads = exchange(
        stat,
        [coef2],
        functools.partial(inner_totals, cells_out, mid),
        [shape((8, mid)), shape((8, mid))],
        4,
    )

    def top(values):
        return values.reshape(n, q, mid)[:, :cols_out]

    rim = top(mid_pre) * coef2[0] + coef2[1]
    rim = (top(mid_up) * coef5[0] + coef5[1] + rim * coef5[2]).astype(BF16)
    rim = lax.ppermute(rim, "height", [(i + 1, i) for i in range(size_h - 1)])
    first_up, g_mid, stat = call(
        functools.partial(conv_back_body, per, px, q),
        "grouped_conv_back",
        (steps,),
        [
            rows_spec(rows, mid),
            rows_spec(rows, mid),
            pl.BlockSpec((per, cols_out, mid), lambda s: (s, 0, 0)),
            planes_spec,
            whole((8, mid)),
            whole((8, mid)),
            whole((8, mid)),
            whole((9, CHUNK, mid)),
        ],
        [planes_spec, whole((9, gw, mid)), whole((2 * mid // LANES, LANES))],
        [shape((n, 4, q, mid)), shape((9, gw, mid), BF16), shape((2 * mid // LANES, LANES))],
        [
            pltpu.VMEM((per, q + 16, mid), BF16),
            pltpu.VMEM((per, q + 16, mid), BF16),
            pltpu.VMEM((16, mid), F32),
            pltpu.VMEM((9, CHUNK, mid), F32),
        ],
        flops=4 * n * q * mid * CHUNK * 9,
        moved=n * q * mid * 8 + n * px * mid * 8,
        vmem=60,
    )(mid_up, mid_pre, rim, pre_planes, coef2, coef5, coef1, wbd)
    coef6, first_grads = exchange(
        stat,
        [coef1],
        functools.partial(inner_totals, cells_in, mid),
        [shape((8, mid)), shape((8, mid))],
        5,
    )

    first_grad, g_first = call(
        first_back_body,
        "first_gradient",
        (steps,),
        [
            rows_spec(per * px, mid),
            rows_spec(per * px, mid),
            whole((8, mid)),
            whole((8, mid)),
            rows_spec(per * px, cin),
        ],
        [rows_spec(per * px, mid), whole((cin, mid))],
        [shape((n * px, mid), BF16), shape((cin, mid), BF16)],
        [pltpu.VMEM((cin, mid), F32)],
        flops=2 * n * px * mid * cin,
        moved=n * px * (mid * 10 + cin * 2),
    )(first_up.reshape(n * px, mid), pre, coef1, coef6, xp)
    head = jnp.concatenate([g_first, g_mid.reshape(9 * gw, mid)], axis=0)
    unit = devices * 16
    lack = -head.shape[0] % unit
    head_sum = split_sum(jnp.pad(head, ((0, lack), (0, 0))))

    grad_images = call(
        functools.partial(image_back_body, per, px, q),
        "image_gradient",
        (steps,),
        [
            rows_spec(per * px, mid),
            whole((cin, mid)),
            rows_spec(rows, cin),
            whole((px, px)),
        ],
        pl.BlockSpec((per, rows_in, cols_in, cin), lambda s: (s, 0, 0, 0)),
        shape((n, rows_in, cols_in, cin), BF16),
        flops=2 * n * px * cin * (mid + px),
        moved=n * px * (mid * 2 + cin * 2) + n * q * cin * 4,
    )(first_grad, w_first, side_back, perm)

    return (
        output.reshape(n, rows_out, cols_out, wide),
        grad_images,
        head_sum[:cin].astype(F32),
        first_grads[1],
        first_grads[0],
        head_sum[cin : cin + 9 * gw].reshape(3, 3, gw, mid).astype(F32),
        mid_grads[1],
        mid_grads[0],
        g_last,
        wide_grads[1],
        wide_grads[0],
        g_side,
        wide_grads[2],
        wide_grads[0],
    )


def solution(mesh):
    split = P("batch", "height", None, None)
    in_specs = (split,) + (P(),) * 12 + (split,)
    out_specs = (split, split) + (P(),) * 12
    return jax.shard_map(
        per_device, mesh=mesh, in_specs=in_specs, out_specs=out_specs, check_vma=False
    )
```

time: 3320 us -> 611 us (0.18)
  local copies, waits for them, and re-layouts: 1350 us -> 18.8 us
  matrix products: 960 us -> 0 us
  blocking collectives: 602 us -> 0 us
  Pallas kernels: 0 us -> 313 us
  other arithmetic: 342 us -> 73.6 us
  waiting for transfers between devices: 7.38 us -> 140 us
  starting transfers between devices: 6.13 us -> 53.2 us
    dot_general x36 -> x0, matrix products: 960 us -> none  [the longest x9 486 us: per_device(): jnp.einsum('bhwgc,bhwgo->cgo', window, mid_grad, preferred_element_type=j...]
    slice x17 -> x7, local copies, waits for them, and re-layouts: 548 us -> 9.53 us  [the longest x1 2.84 us: per_device(): g_last[:, :half]]
    unnamed x1 -> x0, blocking collectives: 361 us -> none
    reshape x20 -> x0, local copies, waits for them, and re-layouts: 338 us -> none  [the longest x8 160 us: per_device(): tap_grad = jnp.einsum('bhwgo,cgo->bhwgc', mid_grad, kernel, preferred_ele...]
    pallas_call x0 -> x15, Pallas kernels: none -> 313 us  [the longest x6 66.3 us: exchange(): pl.pallas_call(functools.partial(exchange_body, epilogue, len(out_shape))...]
    psum x6 -> x0, blocking collectives: 241 us -> none  [the longest x1 42 us: per_device(): first_totals = lax.psum(first_terms, ('batch', 'height'))]
    transpose x8 -> x0, local copies, waits for them, and re-layouts: 200 us -> none  [per_device(): jnp.einsum('bhwgo,cgo->bhwgc', mid_grad, kernel, preferred_element_type=j...]
    ppermute x2 -> x62, waiting for transfers between devices: 7.36 us -> 140 us  [the longest x30 78.6 us: double(): got = lax.ppermute(part, axis, flip(axis, bit))]
  transfers between devices with their start and end apart: 3 -> 62, of which waited for: 1 -> 32; matrix products, arithmetic and copies ran while one was open for 6% -> 8% of each run, Pallas kernels for 0% -> 27%
where the time goes in v1:
time: 611 us; the launch traced here: 602 us
  Pallas kernels  313 us (51%)
  waiting for transfers between devices  140 us (23%)
  other arithmetic  73.6 us (12%)
  starting transfers between devices  53.2 us (9%)
  local copies, waits for them, and re-layouts  18.8 us (3%)
    ppermute x30, waiting for transfers between devices, double(): got = lax.ppermute(part, axis, flip(axis, bit))  78.6 us
    pallas_call x6, Pallas kernels, exchange(): pl.pallas_call(functools.partial(exchange_body, epilogue, len(out_shape))...  66.3 us
    ppermute x30, waiting for transfers between devices, halve(): got = lax.ppermute(send, axis, flip(axis, bit))  56.3 us
    pallas_call x1, Pallas kernels, per_device(): call(functools.partial(image_back_body, per, px, q), 'image_gradient', (s...  48.3 us
    convert_element_type x1, other arithmetic, per_device(): jnp.concatenate([tail_sum[2 * mid:2 * mid + cin], tail_sum[2 * mid + cin:...  36.7 us
    pallas_call x1, Pallas kernels, per_device(): call(functools.partial(conv_back_body, per, px, q), 'grouped_conv_back',...  33.7 us
    pallas_call x1, Pallas kernels, per_device(): call(functools.partial(tail_body, per, q), 'last_gradients', (steps,), [r...  33.4 us
    pallas_call x1, Pallas kernels, per_device(): call(functools.partial(first_body, per, px, q), 'first_product', (steps,)...  31.4 us
  transfers between devices with their start and end apart: 62, of which 32 were waited for; matrix products, arithmetic and copies ran while one was open for 8% of the time, Pallas kernels for 27%

profile of v1, /device:TPU:0, one launch (start us, length us, event | category | flops | bytes accessed | tf_op | source)
XLA Modules:
  0.0 601.6 jit_solution(4044711312847009386)
XLA Ops:
  2.2 5.0 collective-permute-start
  8.5 31.4 %first_product.1 = (bf16[6144,1024]{1,0:T(8,128)(2,1)}, f32[6144,1024]{1,0:T(8,128)}, f32[1536,2048]{1,0:T(8,128)}, f32[48,128]{1,0:T(8,128)}) custom-call(bf16[24,8,32,1024]{3,2,1,0:T(8,128)(2,1)} %img.1, bf16[256,256]{1,0:T(8,128)(2,1)} %fusion.37.perm, bf16[1024,1024]{1,0:T(8,128)(2,1)} %w1.5, bf16[1024,2048]{1,0:T(8,128)(2,1)} %ws.3), custom_call_target="tpu_custom_call" | custom-call | flops 22548578304 | bytes 69206016 | tf_op jit(solution)/shard_map/first_product/pallas_call | solution.py:608
  40.6 12.5 %exchange_0.1 = (f32[8,1024]{1,0:T(8,128)}, f32[8,2048]{1,0:T(8,128)}) custom-call(f32[48,128]{1,0:T(8,128)} %get-tuple-element.46.in_ref, f32[8,1024]{1,0:T(8,128)} %stack.41.rest_0_), custom_call_target="tpu_custom_call" | custom-call | flops 1000 | bytes 100000 | tf_op jit(solution)/shard_map/exchange_0/pallas_call | solution.py:134
  60.2 18.8 %grouped_conv.1 = (f32[1536,1024]{1,0:T(8,128)}, f32[16,128]{1,0:T(8,128)}) custom-call(f32[24,4,64,1024]{3,2,1,0:T(8,128)} %bitcast.38, bf16[24,32,1024]{2,1,0:T(8,128)(2,1)} %copy-done.7, f32[1]{0:T(128)} %bitcast.2.flag, bf16[1024,1024]{1,0:T(8,128)(2,1)} %w1.5, bf16[128,128]{1,0:T(8,128)(2,1)} %fusion.45.perm, f32[8,1024]{1,0:T(8,128)} %get-tuple-element.47.coef.rest_0_, ...), custom_call_target="tpu_custom_call" | custom-call | flops 8858370048 | bytes 31457280 | tf_op jit(solution)/shard_map/grouped_conv/pallas_call | solution.py:644
  79.0 10.5 %exchange_1.1.coef.rest_0_.coef2 = f32[8,1024]{1,0:T(8,128)} custom-call(f32[16,128]{1,0:T(8,128)} %get-tuple-element.49.in_ref, f32[8,1024]{1,0:T(8,128)} %stack.41.rest_0_), custom_call_target="tpu_custom_call" | custom-call | flops 1000 | bytes 100000 | tf_op jit(solution)/shard_map/exchange_1/pallas_call | solution.py:134
  90.3 13.7 %last_product.1 = (bf16[1536,1024]{1,0:T(8,128)(2,1)}, f32[1536,2048]{1,0:T(8,128)}, f32[32,128]{1,0:T(8,128)}) custom-call(f32[1536,1024]{1,0:T(8,128)} %get-tuple-element.48.mid, f32[8,1024]{1,0:T(8,128)} %exchange_1.1.coef.rest_0_.coef2, bf16[1024,2048]{1,0:T(8,128)(2,1)} %wl.1), custom_call_target="tpu_custom_call" | custom-call | flops 6442450944 | bytes 22020096 | tf_op jit(solution)/shard_map/last_product/pallas_call | solution.py:673
  104.0 11.0 %exchange_2.1.coef.rest_0_ = f32[8,2048]{1,0:T(8,128)} custom-call(f32[32,128]{1,0:T(8,128)} %get-tuple-element.52.in_ref, f32[8,2048]{1,0:T(8,128)} %stack.47.rest_0_, f32[8,2048]{1,0:T(8,128)} %get-tuple-element.53.rest_1_), custom_call_target="tpu_custom_call" | custom-call | flops 1000 | bytes 100000 | tf_op jit(solution)/shard_map/exchange_2/pallas_call | solution.py:134
  115.0 17.2 %output.1 = (bf16[1536,2048]{1,0:T(8,128)(2,1)}, f32[48,128]{1,0:T(8,128)}) custom-call(f32[1536,2048]{1,0:T(8,128)} %get-tuple-element.50.last, f32[1536,2048]{1,0:T(8,128)} %get-tuple-element.51.side, bf16[1536,2048]{1,0:T(8,128)(2,1)} %bitcast.42, f32[8,2048]{1,0:T(8,128)} %exchange_2.1.coef.rest_0_), custom_call_target="tpu_custom_call" | custom-call | flops 94371840 | bytes 37748736 | tf_op jit(solution)/shard_map/output/pallas_call | solution.py:693
  132.2 11.6 %exchange_3.1 = (f32[8,2048]{1,0:T(8,128)}, f32[8,2048]{1,0:T(8,128)}) custom-call(f32[48,128]{1,0:T(8,128)} %get-tuple-element.55.in_ref, f32[8,2048]{1,0:T(8,128)} %exchange_2.1.coef.rest_0_), custom_call_target="tpu_custom_call" | custom-call | flops 1000 | bytes 100000 | tf_op jit(solution)/shard_map/exchange_3/pallas_call | solution.py:134
  143.8 33.4 %last_gradients.1 = (bf16[1536,2048]{1,0:T(8,128)(2,1)}, bf16[1536,2048]{1,0:T(8,128)(2,1)}, bf16[1024,2048]{1,0:T(8,128)(2,1)}, bf16[1024,2048]{1,0:T(8,128)(2,1)}) custom-call(f32[1536,2048]{1,0:T(8,128)} %get-tuple-element.50.last, f32[1536,2048]{1,0:T(8,128)} %get-tuple-element.51.side, bf16[1536,2048]{1,0:T(8,128)(2,1)} %bitcast.43, ...), custom_call_target="tpu_custom_call" | custom-call | flops 12884901888 | bytes 58720256 | tf_op jit(solution)/shard_map/last_gradients/pallas_call | solution.py:713
  177.2 21.2 %mid_back.1 = (f32[1536,1024]{1,0:T(8,128)}, f32[1536,1024]{1,0:T(8,128)}, f32[16,128]{1,0:T(8,128)}) custom-call(bf16[1536,2048]{1,0:T(8,128)(2,1)} %get-tuple-element.59.lg, bf16[1536,2048]{1,0:T(8,128)(2,1)} %get-tuple-element.60.sg, bf16[1024,2048]{1,0:T(8,128)(2,1)} %wl.1, bf16[1024,2048]{1,0:T(8,128)(2,1)} %ws.3, f32[1536,1024]{1,0:T(8,128)} %get-tuple-element.48.mid, ...), custom_call_target="tpu_custom_call" | custom-call | flops 12884901888 | bytes 39845888 | tf_op jit(solution)/shard_map/mid_back/pallas_call | solution.py:745
  198.4 11.1 %exchange_4.1 = (f32[8,1024]{1,0:T(8,128)}, f32[8,1024]{1,0:T(8,128)}) custom-call(f32[16,128]{1,0:T(8,128)} %get-tuple-element.62.in_ref, f32[8,1024]{1,0:T(8,128)} %exchange_1.1.coef.rest_0_.coef2), custom_call_target="tpu_custom_call" | custom-call | flops 1000 | bytes 100000 | tf_op jit(solution)/shard_map/exchange_4/pallas_call | solution.py:134
  218.4 5.0 fusion.6
  228.0 5.3 collective-permute-done.1.halo
  234.2 33.7 %grouped_conv_back.1 = (f32[24,4,64,1024]{3,2,1,0:T(8,128)}, bf16[9,32,1024]{2,1,0:T(8,128)(2,1)}, f32[16,128]{1,0:T(8,128)}) custom-call(f32[1536,1024]{1,0:T(8,128)} %get-tuple-element.61.mup, f32[1536,1024]{1,0:T(8,128)} %get-tuple-element.48.mid, bf16[24,16,1024]{2,1,0:T(8,128)(2,1)} %copy-done.18, f32[24,4,64,1024]{3,2,1,0:T(8,128)} %bitcast.39, ...), custom_call_target="tpu_custom_call" | custom-call | flops 14495514624 | bytes 62914560 | tf_op jit(solution)/shard_map/grouped_conv_back/pallas_call | solution.py:777
  267.9 9.7 %exchange_5.1 = (f32[8,1024]{1,0:T(8,128)}, f32[8,1024]{1,0:T(8,128)}) custom-call(f32[16,128]{1,0:T(8,128)} %get-tuple-element.65.in_ref, f32[8,1024]{1,0:T(8,128)} %get-tuple-element.47.coef.rest_0_), custom_call_target="tpu_custom_call" | custom-call | flops 1000 | bytes 100000 | tf_op jit(solution)/shard_map/exchange_5/pallas_call | solution.py:134
  277.6 29.3 %first_gradient.1 = (bf16[6144,1024]{1,0:T(8,128)(2,1)}, bf16[1024,1024]{1,0:T(8,128)(2,1)}) custom-call(f32[6144,1024]{1,0:T(8,128)} %bitcast.40, f32[6144,1024]{1,0:T(8,128)} %get-tuple-element.45.pre, f32[8,1024]{1,0:T(8,128)} %get-tuple-element.47.coef.rest_0_, f32[8,1024]{1,0:T(8,128)} %get-tuple-element.66.back, bf16[6144,1024]{1,0:T(8,128)(2,1)} %get-tuple-element.58.xp), custom_call_target="tpu_custom_call" | custom-call | flops 12884901888 | bytes 75497472 | tf_op jit(solution)/shard_map/first_gradient/pallas_call | solution.py:811
  311.7 48.3 %image_gradient.1 = bf16[24,8,32,1024]{3,2,1,0:T(8,128)(2,1)} custom-call(bf16[6144,1024]{1,0:T(8,128)(2,1)} %get-tuple-element.67.fg, bf16[1024,1024]{1,0:T(8,128)(2,1)} %w1.5, f32[1536,1024]{1,0:T(8,128)} %get-tuple-element.68.side_back, bf16[256,256]{1,0:T(8,128)(2,1)} %fusion.37.perm), custom_call_target="tpu_custom_call" | custom-call | flops 16106127360 | bytes 31457280 | tf_op jit(solution)/shard_map/image_gradient/pallas_call | solution.py:833
  376.1 6.1 %collective-permute-done.23 = bf16[128,1024]{1,0:T(8,128)(2,1)S(1)} collective-permute-done((bf16[128,1024]{1,0:T(8,128)(2,1)S(1)}, bf16[128,1024]{1,0:T(8,128)(2,1)S(1)}, u32[]{:S(2)}, u32[]{:S(2)}) %collective-permute-start.23) | collective-permute-done | bytes 262176 | tf_op jit(solution)/shard_map/ppermute | solution.py:514
  384.7 5.6 add_convert_fusion.1
  397.5 9.9 %collective-permute-done.15 = bf16[32,1024]{1,0:T(8,128)(2,1)S(1)} collective-permute-done((bf16[32,1024]{1,0:T(8,128)(2,1)S(1)}, bf16[32,1024]{1,0:T(8,128)(2,1)S(1)}, u32[]{:S(2)}, u32[]{:S(2)}) %collective-permute-start.15) | collective-permute-done | bytes 65568 | tf_op jit(solution)/shard_map/ppermute | solution.py:514
  443.4 4.9 collective-permute-done.57
  450.5 5.6 collective-permute-done.58
  459.4 5.2 collective-permute-done.30
  468.4 8.5 %collective-permute-done.44 = bf16[192,1024]{1,0:T(8,128)(2,1)S(1)} collective-permute-done((bf16[192,1024]{1,0:T(8,128)(2,1)S(1)}, bf16[192,1024]{1,0:T(8,128)(2,1)S(1)}, u32[]{:S(2)}, u32[]{:S(2)}) %collective-permute-start.44) | collective-permute-done | bytes 393248 | tf_op jit(solution)/shard_map/ppermute | solution.py:514
  479.3 8.9 %collective-permute-done.45 = bf16[96,1024]{1,0:T(8,128)(2,1)S(1)} collective-permute-done((bf16[96,1024]{1,0:T(8,128)(2,1)S(1)}, bf16[96,1024]{1,0:T(8,128)(2,1)S(1)}, u32[]{:S(2)}, u32[]{:S(2)}) %collective-permute-start.45) | collective-permute-done | bytes 196640 | tf_op jit(solution)/shard_map/ppermute | solution.py:514
  498.1 8.8 %collective-permute-done.37 = bf16[48,1024]{1,0:T(8,128)(2,1)S(1)} collective-permute-done((bf16[48,1024]{1,0:T(8,128)(2,1)S(1)}, bf16[48,1024]{1,0:T(8,128)(2,1)S(1)}, u32[]{:S(2)}, u32[]{:S(2)}) %collective-permute-start.37) | collective-permute-done | bytes 98336 | tf_op jit(solution)/shard_map/ppermute | solution.py:521
  516.8 6.7 %collective-permute-done.49 = bf16[192,1024]{1,0:T(8,128)(2,1)S(1)} collective-permute-done((bf16[192,1024]{1,0:T(8,128)(2,1)S(1)}, bf16[192,1024]{1,0:T(8,128)(2,1)S(1)}, u32[]{:S(2)}, u32[]{:S(2)}) %collective-permute-start.49) | collective-permute-done | bytes 393248 | tf_op jit(solution)/shard_map/ppermute | solution.py:521
  527.9 9.4 %collective-permute-done.60 = bf16[256,1024]{1,0:T(8,128)(2,1)S(1)} collective-permute-done((bf16[256,1024]{1,0:T(8,128)(2,1)S(1)}, bf16[256,1024]{1,0:T(8,128)(2,1)S(1)}, u32[]{:S(2)}, u32[]{:S(2)}) %collective-permute-start.60) | collective-permute-done | bytes 524320 | tf_op jit(solution)/shard_map/ppermute | solution.py:521
  539.2 5.6 collective-permute-done.50
  545.3 10.6 %collective-permute-done.40 = bf16[384,1024]{1,0:T(8,128)(2,1)S(1)} collective-permute-done((bf16[384,1024]{1,0:T(8,128)(2,1)S(1)}, bf16[384,1024]{1,0:T(8,128)(2,1)S(1)}, u32[]{:S(2)}, u32[]{:S(2)}) %collective-permute-start.40) | collective-permute-done | bytes 786464 | tf_op jit(solution)/shard_map/ppermute | solution.py:521
  563.9 36.7 %fusion.1 = (f32[1024,2048]{1,0:T(8,128)}, f32[1024,2048]{1,0:T(8,128)}) fusion(bf16[768,1024]{1,0:T(8,128)(2,1)S(1)} %get-tuple-element.80, bf16[768,1024]{1,0:T(8,128)(2,1)S(1)} %get-tuple-element.81, bf16[512,1024]{1,0:T(8,128)(2,1)S(1)} %get-tuple-element.85, bf16[512,1024]{1,0:T(8,128)(2,1)S(1)} %get-tuple-element.84, ...), kind=kLoop, calls=%fused_computation.3 | loop fusion | flops 33554432 | bytes 25165824 | tf_op jit(solution)/shard_map/convert_element_type | solution.py:743
  (294 shorter events, 138.1 us)
Async XLA Ops:
  2.2 56.9 %collective-permute-start = (bf16[24,32,1024]{2,1,0:T(8,128)(2,1)S(1)}, bf16[24,32,1024]{2,1,0:T(8,128)(2,1)S(1)}, u32[]{:S(2)}, u32[]{:S(2)}) collective-permute-start(bf16[24,32,1024]{2,1,0:T(8,128)(2,1)S(1)} %slice_bitcast_fusion), channel_id=1, source_target_pairs={{0,1},{1,2},{2,3},{4,5},{5,6},{6,7},{8,9},{9,10},{10,11},{12,13},{... | collective-permute-start | bytes 4718600 | tf_op jit(solution)/shard_map/ppermute | solution.py:587
  212.7 20.6 %collective-permute-start.1 = (bf16[24,16,1024]{2,1,0:T(8,128)(2,1)S(1)}, bf16[24,16,1024]{2,1,0:T(8,128)(2,1)S(1)}, u32[]{:S(2)}, u32[]{:S(2)}) collective-permute-start(bf16[24,16,1024]{2,1,0:T(8,128)(2,1)S(1)} %fusion.13), channel_id=1, source_target_pairs={{1,0},{2,1},{3,2},{5,4},{6,5},{7,6},{9,8},{10,9},{11,10},{13,12},{... | collective-permute-start | bytes 2359304 | tf_op jit(solution)/shard_map/ppermute | solution.py:776
  223.4 160.2 %collective-permute-start.32 = (bf16[768,1024]{1,0:T(8,128)(2,1)}, bf16[768,1024]{1,0:T(8,128)(2,1)}, u32[]{:S(2)}, u32[]{:S(2)}) collective-permute-start(bf16[768,1024]{1,0:T(8,128)(2,1)} %get-tuple-element.88), channel_id=1, source_target_pairs={{0,4},{4,0},{8,12},{12,8},{16,20},{20,16},{24,28},{28,24},{1,5},{5... | collective-permute-start | bytes 4718600 | tf_op jit(solution)/shard_map/ppermute | solution.py:514
  223.4 161.2 %collective-permute-start.42 = (bf16[768,1024]{1,0:T(8,128)(2,1)}, bf16[768,1024]{1,0:T(8,128)(2,1)}, u32[]{:S(2)}, u32[]{:S(2)}) collective-permute-start(bf16[768,1024]{1,0:T(8,128)(2,1)} %get-tuple-element.89), channel_id=1, source_target_pairs={{0,4},{4,0},{8,12},{12,8},{16,20},{20,16},{24,28},{28,24},{1,5},{5... | collective-permute-start | bytes 4718600 | tf_op jit(solution)/shard_map/ppermute | solution.py:514
  225.0 135.0 %collective-permute-start.52 = (bf16[512,1024]{1,0:T(8,128)(2,1)}, bf16[512,1024]{1,0:T(8,128)(2,1)}, u32[]{:S(2)}, u32[]{:S(2)}) collective-permute-start(bf16[512,1024]{1,0:T(8,128)(2,1)} %constant_dynamic-slice_fusion.4), channel_id=1, source_target_pairs={{0,4},{4,0},{8,12},{12,8},{16,20},{20,16},{24,28},{28,24},{1,5},{5... | collective-permute-start | bytes 3145736 | tf_op jit(solution)/shard_map/ppermute | solution.py:514
  308.9 52.9 %collective-permute-start.12 = (bf16[256,1024]{1,0:T(8,128)(2,1)S(1)}, bf16[256,1024]{1,0:T(8,128)(2,1)}, u32[]{:S(2)}, u32[]{:S(2)}) collective-permute-start(bf16[256,1024]{1,0:T(8,128)(2,1)S(1)} %constant_dynamic-slice_fusion.22), channel_id=1, source_target_pairs={{0,4},{4,0},{8,12},{12,8},{16,20},{20,16},{24,28},{28,24},{1,5},{5... | collective-permute-start | bytes 1572872 | tf_op jit(solution)/shard_map/ppermute | solution.py:514
  309.8 54.0 %collective-permute-start.2 = (bf16[256,1024]{1,0:T(8,128)(2,1)}, bf16[256,1024]{1,0:T(8,128)(2,1)}, u32[]{:S(2)}, u32[]{:S(2)}) collective-permute-start(bf16[256,1024]{1,0:T(8,128)(2,1)} %constant_dynamic-slice_fusion.27), channel_id=1, source_target_pairs={{0,4},{4,0},{8,12},{12,8},{16,20},{20,16},{24,28},{28,24},{1,5},{5... | collective-permute-start | bytes 1572872 | tf_op jit(solution)/shard_map/ppermute | solution.py:514
  361.8 29.8 %collective-permute-start.53 = (bf16[256,1024]{1,0:T(8,128)(2,1)S(1)}, bf16[256,1024]{1,0:T(8,128)(2,1)S(1)}, u32[]{:S(2)}, u32[]{:S(2)}) collective-permute-start(bf16[256,1024]{1,0:T(8,128)(2,1)S(1)} %constant_dynamic-slice_fusion.3), channel_id=1, source_target_pairs={{0,1},{1,0},{2,3},{3,2},{4,5},{5,4},{6,7},{7,6},{8,9},{9,8},{10,11... | collective-permute-start | bytes 1572872 | tf_op jit(solution)/shard_map/ppermute | solution.py:514
  374.7 18.8 %collective-permute-start.14 = (bf16[64,1024]{1,0:T(8,128)(2,1)S(1)}, bf16[64,1024]{1,0:T(8,128)(2,1)S(1)}, u32[]{:S(2)}, u32[]{:S(2)}) collective-permute-start(bf16[64,1024]{1,0:T(8,128)(2,1)S(1)} %constant_dynamic-slice_fusion.20), channel_id=1, source_target_pairs={{0,1},{1,0},{2,3},{3,2},{4,5},{5,4},{6,7},{7,6},{8,9},{9,8},{10,11... | collective-permute-start | bytes 393224 | tf_op jit(solution)/shard_map/ppermute | solution.py:514
  382.2 12.8 %collective-permute-start.4 = (bf16[64,1024]{1,0:T(8,128)(2,1)S(1)}, bf16[64,1024]{1,0:T(8,128)(2,1)S(1)}, u32[]{:S(2)}, u32[]{:S(2)}) collective-permute-start(bf16[64,1024]{1,0:T(8,128)(2,1)S(1)} %constant_dynamic-slice_fusion.25), channel_id=1, source_target_pairs={{0,16},{4,20},{8,24},{12,28},{16,0},{20,4},{24,8},{28,12},{1,17},{... | collective-permute-start | bytes 393224 | tf_op jit(solution)/shard_map/ppermute | solution.py:514
  383.6 12.4 %collective-permute-start.24 = (bf16[64,1024]{1,0:T(8,128)(2,1)S(1)}, bf16[64,1024]{1,0:T(8,128)(2,1)S(1)}, u32[]{:S(2)}, u32[]{:S(2)}) collective-permute-start(bf16[64,1024]{1,0:T(8,128)(2,1)S(1)} %constant_dynamic-slice_fusion.15), channel_id=1, source_target_pairs={{0,2},{1,3},{2,0},{3,1},{4,6},{5,7},{6,4},{7,5},{8,10},{9,11},{10,... | collective-permute-start | bytes 393224 | tf_op jit(solution)/shard_map/ppermute | solution.py:514
  390.3 74.5 %collective-permute-start.43 = (bf16[384,1024]{1,0:T(8,128)(2,1)S(1)}, bf16[384,1024]{1,0:T(8,128)(2,1)S(1)}, u32[]{:S(2)}, u32[]{:S(2)}) collective-permute-start(bf16[384,1024]{1,0:T(8,128)(2,1)S(1)} %constant_dynamic-slice_fusion.8), channel_id=1, source_target_pairs={{0,16},{4,20},{8,24},{12,28},{16,0},{20,4},{24,8},{28,12},{1,17},{... | collective-permute-start | bytes 2359304 | tf_op jit(solution)/shard_map/ppermute | solution.py:514
  391.8 35.2 %collective-permute-start.54 = (bf16[128,1024]{1,0:T(8,128)(2,1)S(1)}, bf16[128,1024]{1,0:T(8,128)(2,1)S(1)}, u32[]{:S(2)}, u32[]{:S(2)}) collective-permute-start(bf16[128,1024]{1,0:T(8,128)(2,1)S(1)} %constant_dynamic-slice_fusion.2), channel_id=1, source_target_pairs={{0,2},{1,3},{2,0},{3,1},{4,6},{5,7},{6,4},{7,5},{8,10},{9,11},{10,... | collective-permute-start | bytes 786440 | tf_op jit(solution)/shard_map/ppermute | solution.py:514
  393.5 72.2 %collective-permute-start.33 = (bf16[384,1024]{1,0:T(8,128)(2,1)S(1)}, bf16[384,1024]{1,0:T(8,128)(2,1)S(1)}, u32[]{:S(2)}, u32[]{:S(2)}) collective-permute-start(bf16[384,1024]{1,0:T(8,128)(2,1)S(1)} %constant_dynamic-slice_fusion.12), channel_id=1, source_target_pairs={{0,8},{4,12},{8,0},{12,4},{16,24},{20,28},{24,16},{28,20},{1,9},{5... | collective-permute-start | bytes 2359304 | tf_op jit(solution)/shard_map/ppermute | solution.py:514
  395.1 12.4 %collective-permute-start.15 = (bf16[32,1024]{1,0:T(8,128)(2,1)S(1)}, bf16[32,1024]{1,0:T(8,128)(2,1)S(1)}, u32[]{:S(2)}, u32[]{:S(2)}) collective-permute-start(bf16[32,1024]{1,0:T(8,128)(2,1)S(1)} %constant_dynamic-slice_fusion.19), channel_id=1, source_target_pairs={{0,2},{1,3},{2,0},{3,1},{4,6},{5,7},{6,4},{7,5},{8,10},{9,11},{10,... | collective-permute-start | bytes 196616 | tf_op jit(solution)/shard_map/ppermute | solution.py:514
  396.1 12.5 %collective-permute-start.5 = (bf16[32,1024]{1,0:T(8,128)(2,1)S(1)}, bf16[32,1024]{1,0:T(8,128)(2,1)S(1)}, u32[]{:S(2)}, u32[]{:S(2)}) collective-permute-start(bf16[32,1024]{1,0:T(8,128)(2,1)S(1)} %constant_dynamic-slice_fusion.24), channel_id=1, source_target_pairs={{0,1},{1,0},{2,3},{3,2},{4,5},{5,4},{6,7},{7,6},{8,9},{9,8},{10,11... | collective-permute-start | bytes 196616 | tf_op jit(solution)/shard_map/ppermute | solution.py:514
  435.5 13.8 %collective-permute-start.29 = (bf16[64,1024]{1,0:T(8,128)(2,1)S(1)}, bf16[64,1024]{1,0:T(8,128)(2,1)S(1)}, u32[]{:S(2)}, u32[]{:S(2)}) collective-permute-start(bf16[64,1024]{1,0:T(8,128)(2,1)S(1)} %pad_maximum_fusion.23), channel_id=1, source_target_pairs={{0,2},{1,3},{2,0},{3,1},{4,6},{5,7},{6,4},{7,5},{8,10},{9,11},{10,... | collective-permute-start | bytes 393224 | tf_op jit(solution)/shard_map/ppermute | solution.py:521
  441.2 15.6 %collective-permute-start.20 = (bf16[128,1024]{1,0:T(8,128)(2,1)S(1)}, bf16[128,1024]{1,0:T(8,128)(2,1)S(1)}, u32[]{:S(2)}, u32[]{:S(2)}) collective-permute-start(bf16[128,1024]{1,0:T(8,128)(2,1)S(1)} %pad_maximum_fusion.16), channel_id=1, source_target_pairs={{0,16},{4,20},{8,24},{12,28},{16,0},{20,4},{24,8},{28,12},{1,17},{... | collective-permute-start | bytes 786440 | tf_op jit(solution)/shard_map/ppermute | solution.py:521
  459.2 99.3 %collective-permute-start.21 = (bf16[256,1024]{1,0:T(8,128)(2,1)S(1)}, bf16[256,1024]{1,0:T(8,128)(2,1)S(1)}, u32[]{:S(2)}, u32[]{:S(2)}) collective-permute-start(bf16[256,1024]{1,0:T(8,128)(2,1)S(1)} %pad_maximum_fusion.10), channel_id=1, source_target_pairs={{0,4},{4,0},{8,12},{12,8},{16,20},{20,16},{24,28},{28,24},{1,5},{5... | collective-permute-start | bytes 1572872 | tf_op jit(solution)/shard_map/ppermute | solution.py:521
  464.6 94.1 %collective-permute-start.11 = (bf16[256,1024]{1,0:T(8,128)(2,1)S(1)}, bf16[256,1024]{1,0:T(8,128)(2,1)S(1)}, u32[]{:S(2)}, u32[]{:S(2)}) collective-permute-start(bf16[256,1024]{1,0:T(8,128)(2,1)S(1)} %pad_maximum_fusion.9), channel_id=1, source_target_pairs={{0,4},{4,0},{8,12},{12,8},{16,20},{20,16},{24,28},{28,24},{1,5},{5... | collective-permute-start | bytes 1572872 | tf_op jit(solution)/shard_map/ppermute | solution.py:521
  464.8 91.7 %collective-permute-start.31 = (bf16[256,1024]{1,0:T(8,128)(2,1)S(1)}, bf16[256,1024]{1,0:T(8,128)(2,1)S(1)}, u32[]{:S(2)}, u32[]{:S(2)}) collective-permute-start(bf16[256,1024]{1,0:T(8,128)(2,1)S(1)} %pad_maximum_fusion.11), channel_id=1, source_target_pairs={{0,4},{4,0},{8,12},{12,8},{16,20},{20,16},{24,28},{28,24},{1,5},{5... | collective-permute-start | bytes 1572872 | tf_op jit(solution)/shard_map/ppermute | solution.py:521
  465.7 11.1 %collective-permute-start.44 = (bf16[192,1024]{1,0:T(8,128)(2,1)S(1)}, bf16[192,1024]{1,0:T(8,128)(2,1)S(1)}, u32[]{:S(2)}, u32[]{:S(2)}) collective-permute-start(bf16[192,1024]{1,0:T(8,128)(2,1)S(1)} %constant_dynamic-slice_fusion.7), channel_id=1, source_target_pairs={{0,1},{1,0},{2,3},{3,2},{4,5},{5,4},{6,7},{7,6},{8,9},{9,8},{10,11... | collective-permute-start | bytes 1179656 | tf_op jit(solution)/shard_map/ppermute | solution.py:514
  477.0 11.2 %collective-permute-start.45 = (bf16[96,1024]{1,0:T(8,128)(2,1)S(1)}, bf16[96,1024]{1,0:T(8,128)(2,1)S(1)}, u32[]{:S(2)}, u32[]{:S(2)}) collective-permute-start(bf16[96,1024]{1,0:T(8,128)(2,1)S(1)} %constant_dynamic-slice_fusion.6), channel_id=1, source_target_pairs={{0,2},{1,3},{2,0},{3,1},{4,6},{5,7},{6,4},{7,5},{8,10},{9,11},{10,... | collective-permute-start | bytes 589832 | tf_op jit(solution)/shard_map/ppermute | solution.py:514
  477.5 11.1 %collective-permute-start.35 = (bf16[96,1024]{1,0:T(8,128)(2,1)S(1)}, bf16[96,1024]{1,0:T(8,128)(2,1)S(1)}, u32[]{:S(2)}, u32[]{:S(2)}) collective-permute-start(bf16[96,1024]{1,0:T(8,128)(2,1)S(1)} %constant_dynamic-slice_fusion.10), channel_id=1, source_target_pairs={{0,1},{1,0},{2,3},{3,2},{4,5},{5,4},{6,7},{7,6},{8,9},{9,8},{10,11... | collective-permute-start | bytes 589832 | tf_op jit(solution)/shard_map/ppermute | solution.py:514
  495.0 11.9 %collective-permute-start.37 = (bf16[48,1024]{1,0:T(8,128)(2,1)S(1)}, bf16[48,1024]{1,0:T(8,128)(2,1)S(1)}, u32[]{:S(2)}, u32[]{:S(2)}) collective-permute-start(bf16[48,1024]{1,0:T(8,128)(2,1)S(1)} %add_convert_fusion.22), channel_id=1, source_target_pairs={{0,2},{1,3},{2,0},{3,1},{4,6},{5,7},{6,4},{7,5},{8,10},{9,11},{10,... | collective-permute-start | bytes 294920 | tf_op jit(solution)/shard_map/ppermute | solution.py:521
  498.0 13.0 %collective-permute-start.48 = (bf16[96,1024]{1,0:T(8,128)(2,1)S(1)}, bf16[96,1024]{1,0:T(8,128)(2,1)S(1)}, u32[]{:S(2)}, u32[]{:S(2)}) collective-permute-start(bf16[96,1024]{1,0:T(8,128)(2,1)S(1)} %pad_maximum_fusion.20), channel_id=1, source_target_pairs={{0,2},{1,3},{2,0},{3,1},{4,6},{5,7},{6,4},{7,5},{8,10},{9,11},{10,... | collective-permute-start | bytes 589832 | tf_op jit(solution)/shard_map/ppermute | solution.py:521
  511.1 12.4 %collective-permute-start.49 = (bf16[192,1024]{1,0:T(8,128)(2,1)S(1)}, bf16[192,1024]{1,0:T(8,128)(2,1)S(1)}, u32[]{:S(2)}, u32[]{:S(2)}) collective-permute-start(bf16[192,1024]{1,0:T(8,128)(2,1)S(1)} %pad_maximum_fusion.14), channel_id=1, source_target_pairs={{0,1},{1,0},{2,3},{3,2},{4,5},{5,4},{6,7},{7,6},{8,9},{9,8},{10,11... | collective-permute-start | bytes 1179656 | tf_op jit(solution)/shard_map/ppermute | solution.py:521
  515.3 11.0 %collective-permute-start.39 = (bf16[192,1024]{1,0:T(8,128)(2,1)S(1)}, bf16[192,1024]{1,0:T(8,128)(2,1)S(1)}, u32[]{:S(2)}, u32[]{:S(2)}) collective-permute-start(bf16[192,1024]{1,0:T(8,128)(2,1)S(1)} %pad_maximum_fusion.13), channel_id=1, source_target_pairs={{0,16},{4,20},{8,24},{12,28},{16,0},{20,4},{24,8},{28,12},{1,17},{... | collective-permute-start | bytes 1179656 | tf_op jit(solution)/shard_map/ppermute | solution.py:521
  523.5 13.8 %collective-permute-start.60 = (bf16[256,1024]{1,0:T(8,128)(2,1)S(1)}, bf16[256,1024]{1,0:T(8,128)(2,1)S(1)}, u32[]{:S(2)}, u32[]{:S(2)}) collective-permute-start(bf16[256,1024]{1,0:T(8,128)(2,1)S(1)} %pad_maximum_fusion.12), channel_id=1, source_target_pairs={{0,1},{1,0},{2,3},{3,2},{4,5},{5,4},{6,7},{7,6},{8,9},{9,8},{10,11... | collective-permute-start | bytes 1572872 | tf_op jit(solution)/shard_map/ppermute | solution.py:521
  526.3 18.5 %collective-permute-start.50 = (bf16[384,1024]{1,0:T(8,128)(2,1)S(1)}, bf16[384,1024]{1,0:T(8,128)(2,1)S(1)}, u32[]{:S(2)}, u32[]{:S(2)}) collective-permute-start(bf16[384,1024]{1,0:T(8,128)(2,1)S(1)} %pad_maximum_fusion.7), channel_id=1, source_target_pairs={{0,16},{4,20},{8,24},{12,28},{16,0},{20,4},{24,8},{28,12},{1,17},{... | collective-permute-start | bytes 2359304 | tf_op jit(solution)/shard_map/ppermute | solution.py:521
  537.3 18.6 %collective-permute-start.40 = (bf16[384,1024]{1,0:T(8,128)(2,1)S(1)}, bf16[384,1024]{1,0:T(8,128)(2,1)S(1)}, u32[]{:S(2)}, u32[]{:S(2)}) collective-permute-start(bf16[384,1024]{1,0:T(8,128)(2,1)S(1)} %pad_maximum_fusion.6), channel_id=1, source_target_pairs={{0,8},{4,12},{8,0},{12,4},{16,24},{20,28},{24,16},{28,20},{1,9},{5... | collective-permute-start | bytes 2359304 | tf_op jit(solution)/shard_map/ppermute | solution.py:521
  544.8 16.8 %collective-permute-start.61 = (bf16[512,1024]{1,0:T(8,128)(2,1)S(1)}, bf16[512,1024]{1,0:T(8,128)(2,1)S(1)}, u32[]{:S(2)}, u32[]{:S(2)}) collective-permute-start(bf16[512,1024]{1,0:T(8,128)(2,1)S(1)} %pad_maximum_fusion.5), channel_id=1, source_target_pairs={{0,4},{4,0},{8,12},{12,8},{16,20},{20,16},{24,28},{28,24},{1,5},{5... | collective-permute-start | bytes 3145736 | tf_op jit(solution)/shard_map/ppermute | solution.py:521
  (49 other events, 843.6 us)
